TPU v7x, 128 devices: a whole 4x4x4 slice. The times are simulated.
128 devices in a mesh: row: 8 (over y, core), col: 16 (over x, z).
Axes of the slice: x: 4, y: 4, z: 4, core: 2. Of those that a mesh axis runs over, the one named last changes fastest.
Arguments:
- object_slab: float32 [2, 4096, 8192], P(None, 'row', 'col'), may hold values from -15 to 15
- probe_field: float32 [2, 4, 256, 256], replicated, may hold values from -6 to 6
- patterns: float32 [128, 4, 256, 256], P(('row', 'col')), may hold values from 0 to 3
- offsets: int32 [128, 4, 2], P(('row', 'col')), may hold values from 0 to 511
- counts: int32 [128], replicated, may hold values from 1 to 4, 176 in all
Outputs:
- new_object: float32 [2, 4096, 8192], P(None, 'row', 'col')
- new_probe: float32 [2, 4, 256, 256], replicated
- loss_mean: float32 [], replicated
Inputs may be any that keep to these rules, and one draw needn't show every extreme that they name: The counts sum to 176; some tile owns exactly 4 positions. `offsets`: only the first counts[t] slots of tile t are scan positions.
All inputs are finite; a program needn't handle non-finite values.
Results may differ from a plain program's by a relative error of at most 0.0003.
Values sent between devices are 32-bit elements; how exact they have to be, the bound alone decides.
A program may use at most 128 MiB of HBM per device.

v0:
```python
import math

import jax
import jax.numpy as jnp
from jax import lax
from jax.sharding import PartitionSpec as P


def shifted(shard, axis, by):
    size = lax.axis_size(axis)
    pairs = [(i, i + by) for i in range(size) if 0 <= i + by < size]
    return lax.ppermute(shard, axis, pairs)


def fourier_tables(pixels):
    counter = jnp.arange(pixels, dtype=jnp.int32)
    phases = counter[:, None] * counter[None, :] % pixels
    angles = phases.astype(jnp.float32) * (2.0 * math.pi / pixels)
    factor = 1.0 / math.sqrt(pixels)
    return (jnp.cos(angles) * factor, -jnp.sin(angles) * factor)


def transform(wave_re, wave_im, table_re, table_im):
    highest = lax.Precision.HIGHEST
    left_re = jnp.einsum("kn,mnj->mkj", table_re, wave_re, precision=highest) - jnp.einsum(
        "kn,mnj->mkj", table_im, wave_im, precision=highest
    )
    left_im = jnp.einsum("kn,mnj->mkj", table_re, wave_im, precision=highest) + jnp.einsum(
        "kn,mnj->mkj", table_im, wave_re, precision=highest
    )
    right_re = jnp.einsum("mkn,nj->mkj", left_re, table_re, precision=highest) - jnp.einsum(
        "mkn,nj->mkj", left_im, table_im, precision=highest
    )
    right_im = jnp.einsum("mkn,nj->mkj", left_re, table_im, precision=highest) + jnp.einsum(
        "mkn,nj->mkj", left_im, table_re, precision=highest
    )
    return (right_re, right_im)


def process(obj_patch, pattern, probe_field, table_re, table_im):
    patch_re = obj_patch[0]
    patch_im = obj_patch[1]
    probe_re = probe_field[0]
    probe_im = probe_field[1]
    exit_re = probe_re * patch_re - probe_im * patch_im
    exit_im = probe_re * patch_im + probe_im * patch_re
    spec_re, spec_im = transform(exit_re, exit_im, table_re, table_im)
    intensity = jnp.sum(spec_re * spec_re + spec_im * spec_im, axis=0)
    residual = intensity - pattern
    back_re, back_im = transform(residual * spec_re, residual * spec_im, table_re, -table_im)
    grad_re = jnp.sum(probe_re * back_re + probe_im * back_im, axis=0)
    grad_im = jnp.sum(probe_re * back_im - probe_im * back_re, axis=0)
    modes_re = patch_re * back_re + patch_im * back_im
    modes_im = patch_re * back_im - patch_im * back_re
    return (
        jnp.stack([grad_re, grad_im]),
        jnp.stack([modes_re, modes_im]),
        0.5 * jnp.sum(residual * residual),
    )


def body(object_slab, probe_field, patterns, offsets, counts):
    tile_cells = object_slab.shape[1]
    pixels = probe_field.shape[2]
    table_re, table_im = fourier_tables(pixels)
    slot_patterns = patterns[0]
    slot_offsets = offsets[0]
    from_right = shifted(object_slab[:, :, :pixels], "col", -1)
    widened = jnp.concatenate([object_slab, from_right], axis=2)
    from_below = shifted(widened[:, :pixels, :], "row", -1)
    extended = jnp.concatenate([widened, from_below], axis=1)
    device_id = lax.axis_index(("row", "col"))
    own_count = lax.dynamic_index_in_dim(counts, device_id, 0, keepdims=False)

    def patch_at(slot_index):
        row_at = slot_offsets[slot_index, 0]
        col_at = slot_offsets[slot_index, 1]
        return (
            row_at,
            col_at,
            lax.dynamic_slice(extended, (0, row_at, col_at), (2, pixels, pixels)),
        )

    def add_patch(grad_ext, gradient, row_at, col_at):
        current = lax.dynamic_slice(grad_ext, (0, row_at, col_at), (2, pixels, pixels))
        return lax.dynamic_update_slice(grad_ext, current + gradient, (0, row_at, col_at))

    def own_slot(slot_index, carried):
        grad_ext, grad_probe, loss_sum = carried
        row_at, col_at, obj_patch = patch_at(slot_index)
        gradient, modes_grad, partial_loss = process(
            obj_patch, slot_patterns[slot_index], probe_field, table_re, table_im
        )
        return (
            add_patch(grad_ext, gradient, row_at, col_at),
            grad_probe + modes_grad,
            loss_sum + partial_loss,
        )

    start = (
        jnp.zeros(extended.shape, jnp.float32),
        jnp.zeros(probe_field.shape, jnp.float32),
        jnp.zeros((), jnp.float32),
    )
    grad_ext, grad_probe, loss_sum = lax.fori_loop(0, own_count, own_slot, start)
    from_above = shifted(grad_ext[:, tile_cells:, :], "row", 1)
    upper = grad_ext[:, :tile_cells, :].at[:, :pixels, :].add(from_above)
    from_left = shifted(upper[:, :, tile_cells:], "col", 1)
    object_grad = upper[:, :, :tile_cells].at[:, :, :pixels].add(from_left)
    probe_peak = jnp.max(
        jnp.sum(probe_field[0] * probe_field[0] + probe_field[1] * probe_field[1], axis=0)
    )
    new_object = object_slab - object_grad / probe_peak
    local_peak = jnp.max(object_slab[0] * object_slab[0] + object_slab[1] * object_slab[1])
    largest = lax.pmax(local_peak, ("row", "col"))
    scans = jnp.sum(counts).astype(jnp.float32) * (pixels * pixels)
    probe_total, loss_total = lax.psum((grad_probe, loss_sum), ("row", "col"))
    new_probe = probe_field - probe_total / largest
    return (new_object, new_probe, loss_total / scans)


def solution(mesh):
    placed = (
        P(None, "row", "col"),
        P(),
        P(("row", "col"), None, None, None),
        P(("row", "col"), None, None),
        P(),
    )
    return jax.shard_map(
        body,
        mesh=mesh,
        in_specs=placed,
        out_specs=(P(None, "row", "col"), P(), P()),
        check_vma=False,
    )
```

profile of v0, /device:TPU:1, one launch (start us, length us, event | category | flops | bytes accessed | tf_op | source)
XLA Modules:
  0.0 522.2 jit_solution(12385859606634244426)
XLA Ops:
  10.1 25.7 %collective-permute-done = f32[2,512,256]{2,1,0:T(8,128)S(1)} collective-permute-done((f32[2,512,256]{2,1,0:T(8,128)S(1)}, f32[2,512,256]{2,1,0:T(8,128)S(1)}, u32[]{:S(2)}, u32[]{:S(2)}) %collective-permute-start) | collective-permute-done | bytes 1048608 | tf_op jit(solution)/shard_map/ppermute | solution.py:12
  37.7 3.2 collective-permute-start.1
  41.5 18.7 %collective-permute-done.1 = f32[2,256,768]{2,1,0:T(8,128)S(1)} collective-permute-done((f32[2,256,768]{2,1,0:T(8,128)S(1)}, f32[2,256,768]{2,1,0:T(8,128)S(1)}, u32[]{:S(2)}, u32[]{:S(2)}) %collective-permute-start.1) | collective-permute-done | bytes 1572896 | tf_op jit(solution)/shard_map/ppermute | solution.py:12
  60.2 4.4 pad_maximum_fusion
  64.5 2.4 broadcast_in_dim.4
  69.3 70.6 %while.19 = (s32[]{:T(128)}, f32[2,768,768]{2,1,0:T(8,128)}, f32[2,4,256,256]{3,2,1,0:T(8,128)}, f32[]{:T(128)}, s32[]{:T(128)}, /*index=5*/s32[4,2]{0,1:T(2,128...) while((s32[]{:T(128)}, f32[2,768,768]{2,1,0:T(8,128)}, ...), condition=%wide.region_5.6_spmd.clone.clone, body=%wide.region_0.5_spmd.clone.clone.sunk | while | flops 12913803264 | bytes 83886480 | solution.py:105
  76.3 2.7 fusion.235
  79.1 2.8 fusion.236
  81.8 2.8 fusion.232
  84.6 2.8 fusion.233
  87.4 3.1 fusion.234
  90.4 2.7 convolution_subtract_fusion.6
  93.1 2.7 fusion.237
  95.8 2.7 add_reduce_fusion.4
  99.5 2.8 fusion.242
  102.4 2.7 fusion.243
  105.1 2.7 fusion.239
  107.7 2.7 fusion.240
  110.4 2.7 fusion.241
  113.1 3.0 convolution_subtract_fusion.7
  116.1 2.7 fusion.244
  118.8 3.3 add_bitcast_fusion.2
  125.2 6.5 %dynamic_update_slice.7 = f32[2,768,768]{2,1,0:T(8,128)} dynamic-update-slice(f32[2,768,768]{2,1,0:T(8,128)} %get-tuple-element.369, f32[2,256,256]{2,1,0:T(8,128)S(1)} %maximum_add_fusion.4, s32[]{:T(128)} %constant.101.clone.1..sunk, s32[]{:T(128)S(6)} %select_n.176, s32[]{:T(128)S(6)} %select_n.177) | dynamic-update-slice | bytes 1048580 | tf_op jit(solution)/shard_map/while/body/dynamic_update_slice | solution.py:86
  139.9 2.7 slice.104
  144.6 2.1 slice.102
  146.7 15.5 %collective-permute-done.2 = f32[2,256,768]{2,1,0:T(8,128)} collective-permute-done((f32[2,256,768]{2,1,0:T(8,128)}, f32[2,256,768]{2,1,0:T(8,128)}, u32[]{:S(2)}, u32[]{:S(2)}) %collective-permute-start.2) | collective-permute-done | bytes 1572896 | tf_op jit(solution)/shard_map/ppermute | solution.py:12
  162.2 2.1 add_dynamic-update-slice_fusion
  167.0 133.3 %collective-permute-start.3 = (f32[2,512,256]{2,1,0:T(8,128)}, f32[2,512,256]{2,1,0:T(8,128)S(1)}, u32[]{:S(2)}, u32[]{:S(2)}) collective-permute-start(f32[2,512,256]{2,1,0:T(8,128)} %slice.123), channel_id=1, source_target_pairs={{0,1},{1,2},{2,3},{3,4},{4,5},{5,6},{6,7},{7,8},{8,9},{9,10},{10,1... | collective-permute-start | bytes 3145736 | tf_op jit(solution)/shard_map/ppermute | solution.py:12
  301.2 136.6 %pmax.7 = f32[]{:T(128)} all-reduce(f32[]{:T(128)} %add_reduce_fusion.1), channel_id=1, replica_groups=mesh['row'=8,'col'=16] {'row','col'}, use_global_device_ids=true, to_apply=%region_10.11 | all-reduce | flops 1 | bytes 8 | tf_op jit(solution)/shard_map/pmax | solution.py:115
  439.9 65.0 %psum.15 = f32[]{:T(128)} all-reduce(f32[]{:T(128)} %get-tuple-element.178), channel_id=1, replica_groups=mesh['row'=8,'col'=16] {'row','col'}, use_global_device_ids=true, to_apply=%region_11.12 | all-reduce | flops 1 | bytes 8 | tf_op jit(solution)/shard_map/psum | solution.py:117
  505.6 4.1 divide_subtract_fusion
  511.6 2.4 divide_subtract_fusion.1
  (47 shorter events, 24.6 us)
Async XLA Ops:
  7.2 2.8 copy-start.3
  7.2 498.4 %all-reduce.2.cloned.1.call-start = ((), (), s32[]{:S(2)}) async-start(), calls=%async_computation | async-start | bytes 4194304 | tf_op jit(solution)/shard_map/psum | solution.py:117
  8.7 27.2 %collective-permute-start = (f32[2,512,256]{2,1,0:T(8,128)S(1)}, f32[2,512,256]{2,1,0:T(8,128)S(1)}, u32[]{:S(2)}, u32[]{:S(2)}) collective-permute-start(f32[2,512,256]{2,1,0:T(8,128)S(1)} %slice.100), channel_id=1, source_target_pairs={{1,0},{2,1},{3,2},{4,3},{5,4},{6,5},{7,6},{8,7},{9,8},{10,9},{11,1... | collective-permute-start | bytes 3145736 | tf_op jit(solution)/shard_map/ppermute | solution.py:12
  36.0 1.7 copy-start.8
  37.6 3.3 copy-start.10
  37.7 22.4 %collective-permute-start.1 = (f32[2,256,768]{2,1,0:T(8,128)S(1)}, f32[2,256,768]{2,1,0:T(8,128)S(1)}, u32[]{:S(2)}, u32[]{:S(2)}) collective-permute-start(f32[2,256,768]{2,1,0:T(8,128)S(1)} %slice.120), channel_id=1, source_target_pairs={{16,0},{32,16},{48,32},{64,48},{80,64},{96,80},{112,96},{17,1},{33... | collective-permute-start | bytes 4718600 | tf_op jit(solution)/shard_map/ppermute | solution.py:12
  66.9 2.3 copy-start
  66.9 2.3 copy-start.9
  118.7 3.3 copy-start.1
  122.5 1.3 copy-start.2
  142.5 19.7 %collective-permute-start.2 = (f32[2,256,768]{2,1,0:T(8,128)}, f32[2,256,768]{2,1,0:T(8,128)}, u32[]{:S(2)}, u32[]{:S(2)}) collective-permute-start(f32[2,256,768]{2,1,0:T(8,128)} %slice.104), channel_id=1, source_target_pairs={{0,16},{16,32},{32,48},{48,64},{64,80},{80,96},{96,112},{1,17},{17... | collective-permute-start | bytes 4718600 | tf_op jit(solution)/shard_map/ppermute | solution.py:12
  164.3 1.7 copy-start.6
  166.0 134.4 %copy-start.4 = (f32[2,512,512]{2,1,0:T(8,128)S(1)}, f32[2,512,512]{2,1,0:T(8,128)}, u32[]{:S(2)}) copy-start(f32[2,512,512]{2,1,0:T(8,128)} %param.11) | copy-start | bytes 6291460
  167.0 343.0 %collective-permute-start.3 = (f32[2,512,256]{2,1,0:T(8,128)}, f32[2,512,256]{2,1,0:T(8,128)S(1)}, u32[]{:S(2)}, u32[]{:S(2)}) collective-permute-start(f32[2,512,256]{2,1,0:T(8,128)} %slice.123), channel_id=1, source_target_pairs={{0,1},{1,2},{2,3},{3,4},{4,5},{5,6},{6,7},{7,8},{8,9},{9,10},{10,1... | collective-permute-start | bytes 3145736 | tf_op jit(solution)/shard_map/ppermute | solution.py:12
  505.6 4.1 copy-start.7
  510.0 1.6 copy-start.5
Sparse Core Ops, SparseCore 0:
  144.7 346.2 all-reduce.1
where the time goes:
time: 524 us; the launch traced here: 522 us
  blocking collectives  202 us (39%)
  starting transfers between devices  140 us (27%)
  waiting for transfers between devices  60 us (11%)
  matrix products  44.6 us (9%)
  local copies, waits for them, and re-layouts  27.7 us (5%)
  other arithmetic  20.1 us (4%)
  between operations  16.8 us (3%)
  loops' own time  11.6 us (2%)
    ppermute x4, starting transfers between devices, shifted(): return lax.ppermute(shard, axis, pairs)  140 us
    pmax x1, blocking collectives, body(): largest = lax.pmax(local_peak, ('row', 'col'))  137 us
    psum x1, blocking collectives, body(): probe_total, loss_total = lax.psum((grad_probe, loss_sum), ('row', 'col'))  65 us
    ppermute x4, waiting for transfers between devices, shifted(): return lax.ppermute(shard, axis, pairs)  59.9 us
    another operation x1, loops' own time, body(): lax.fori_loop(0, own_count, own_slot, start)  11.6 us
  transfers between devices with their start and end apart: 5, of which 3 were waited for; matrix products, arithmetic and copies ran while one was open for 2% of the time, Pallas kernels for 0%

commit v1 on v0

v1 whole, which is shorter than its diff:
```python
import math

import jax
import jax.numpy as jnp
import ml_dtypes
import numpy as np
from jax import lax
from jax.experimental import pallas as pl
from jax.experimental.pallas import tpu as pltpu
from jax.sharding import PartitionSpec as P

N = 256
H = 128

def split(x):
    hi = x.astype(jnp.bfloat16)
    lo = (x - hi.astype(jnp.float32)).astype(jnp.bfloat16)
    return hi, lo

def tables():
    k = np.arange(H)[:, None]
    n = np.arange(H)[None, :]
    out = []
    for q in (0, 1):
        ph = -2.0 * math.pi * ((n * (2 * k + q)) % N) / N
        c, s = np.cos(ph) / 16.0, np.sin(ph) / 16.0
        out.append(np.block([[c, -s], [s, c]]))
    t = np.stack(out).astype(np.float32)
    def hl(a):
        hi = a.astype(ml_dtypes.bfloat16)
        lo = (a - hi.astype(np.float32)).astype(ml_dtypes.bfloat16)
        return hi, lo
    hi, lo = hl(t)
    left = np.concatenate([hi, hi, lo], axis=2)
    hiT, loT = hi.transpose(0, 2, 1), lo.transpose(0, 2, 1)
    leftT = np.concatenate([hiT, hiT, loT], axis=2)
    right = np.concatenate([hi, hi, lo], axis=1)
    rightT = np.concatenate([hiT, hiT, loT], axis=1)
    perm = np.zeros((N, N), np.float32)
    for i in range(H):
        perm[2 * i, i] = 1; perm[2 * i + 1, H + i] = 1
    return left, leftT, right, rightT, perm.astype(ml_dtypes.bfloat16)

def dot(a, b):
    return jnp.dot(a, b, preferred_element_type=jnp.float32)

def lmul(t, x):
    hi, lo = split(x)
    return dot(t, jnp.concatenate([hi, lo, hi], axis=0))

def rmul(x, t):
    hi, lo = split(x)
    return dot(jnp.concatenate([hi, lo, hi], axis=1), t)

def compute_kernel(count_ref, off_ref, ext, probe, pat, left, leftT, right, rightT, perm,
                   gext, pgrad, loss_ref, patch, psi, res, acc, swap):
    gext[...] = jnp.zeros_like(gext)
    pgrad[...] = jnp.zeros_like(pgrad)
    loss_ref[...] = jnp.zeros_like(loss_ref)

    def slot(s, _):
        r = off_ref[2 * s]
        c = off_ref[2 * s + 1]
        ca = pl.multiple_of(c // 128 * 128, 128)
        cs = c - ca
        ra = pl.multiple_of(r // 8 * 8, 8)
        rs = r - ra
        for comp in (0, 1):
            x = ext[comp, pl.ds(ra, 264), pl.ds(ca, 384)]
            x = pltpu.roll(x, 384 - cs, 1)[:, :N]
            patch[comp] = pltpu.roll(x, 264 - rs, 0)[:N]
        hi, lo = split(pat[s])
        y = dot(hi, perm[...]) + dot(lo, perm[...])
        for q in (0, 1):
            swap[q] = y[:, q * H:(q + 1) * H]
        for q in (0, 1):
            for p in (0, 1):
                res[q, p * H:(p + 1) * H, :] = -swap[q, pl.ds(p, H, stride=2), :]

        def fwd(m, _):
            qr, qi, orr, oi = probe[0, m], probe[1, m], patch[0], patch[1]
            er = qr * orr - qi * oi
            ei = qr * oi + qi * orr
            L = []
            for p in (0, 1):
                f = (lambda a: a[:H] + a[H:]) if p == 0 else (lambda a: a[:H] - a[H:])
                L.append(lmul(left[p], jnp.concatenate([f(er), f(ei)], axis=0)))
            re = jnp.concatenate([L[0][:H], L[1][:H]], axis=0)
            im = jnp.concatenate([L[0][H:], L[1][H:]], axis=0)
            for q in (0, 1):
                f = (lambda a: a[:, :H] + a[:, H:]) if q == 0 else (lambda a: a[:, :H] - a[:, H:])
                x = rmul(jnp.concatenate([f(re), f(im)], axis=1), rightT[q])
                psi[m, q] = x
                res[q] += x[:, :H] * x[:, :H] + x[:, H:] * x[:, H:]
            return 0
        lax.fori_loop(0, 4, fwd, 0)
        loss_ref[...] += jnp.sum((res[0] * res[0] + res[1] * res[1]).reshape(32, 8, 128), axis=0)
        acc[...] = jnp.zeros_like(acc)

        def bwd(m, _):
            t = []
            for q in (0, 1):
                R = res[q]
                t.append(rmul(psi[m, q] * jnp.concatenate([R, R], axis=1), right[q]))
            x0, x1 = t[0] + t[1], t[0] - t[1]
            L = []
            for p in (0, 1):
                sl = slice(p * H, (p + 1) * H)
                y = jnp.concatenate([
                    jnp.concatenate([x0[sl, :H], x1[sl, :H]], axis=1),
                    jnp.concatenate([x0[sl, H:], x1[sl, H:]], axis=1)], axis=0)
                L.append(lmul(leftT[p], y))
            top, bot = L[0] + L[1], L[0] - L[1]
            for i, b in enumerate((top, bot)):
                sl = slice(i * H, (i + 1) * H)
                br, bi = b[:H], b[H:]
                qr, qi = probe[0, m, sl], probe[1, m, sl]
                orr, oi = patch[0, sl], patch[1, sl]
                acc[0, sl, :N] += qr * br + qi * bi
                acc[1, sl, :N] += qr * bi - qi * br
                pgrad[0, m, sl] += orr * br + oi * bi
                pgrad[1, m, sl] += orr * bi - oi * br
            return 0
        lax.fori_loop(0, 4, bwd, 0)
        for comp in (0, 1):
            x = pltpu.roll(acc[comp], rs, 0)
            gext[comp, pl.ds(ra, 264), pl.ds(ca, 384)] += pltpu.roll(x, cs, 1)
        return 0

    lax.fori_loop(0, count_ref[0], slot, 0)

def compute(count, offs, ext, probe, pat):
    left, leftT, right, rightT, perm = [jnp.asarray(t) for t in tables()]
    V = pl.BlockSpec(memory_space=pltpu.VMEM)
    S = pl.BlockSpec(memory_space=pltpu.SMEM)
    return pl.pallas_call(
        compute_kernel,
        out_shape=(jax.ShapeDtypeStruct((2, 776, 896), jnp.float32),
                   jax.ShapeDtypeStruct((2, 4, N, N), jnp.float32),
                   jax.ShapeDtypeStruct((8, 128), jnp.float32)),
        in_specs=[S, S] + [V] * 8,
        out_specs=(V, V, V),
        scratch_shapes=[pltpu.VMEM((2, N, N), jnp.float32), pltpu.VMEM((4, 2, N, N), jnp.float32),
                        pltpu.VMEM((2, N, H), jnp.float32), pltpu.VMEM((2, 264, 384), jnp.float32),
                        pltpu.VMEM((2, N, H), jnp.float32)],
        compiler_params=pltpu.CompilerParams(vmem_limit_bytes=56 << 20),
        name="compute",
    )(count, offs, ext, probe, pat, left, leftT, right, rightT, perm)


def shifted(shard, axis, by):
    size = lax.axis_size(axis)
    pairs = [(i, i + by) for i in range(size) if 0 <= i + by < size]
    return lax.ppermute(shard, axis, pairs)


def body(object_slab, probe_field, patterns, offsets, counts):
    tile = object_slab.shape[1]
    pixels = probe_field.shape[2]
    from_right = shifted(object_slab[:, :, :pixels], "col", -1)
    widened = jnp.concatenate([object_slab, from_right], axis=2)
    from_below = shifted(widened[:, :pixels, :], "row", -1)
    extended = jnp.concatenate([widened, from_below], axis=1)
    extended = jnp.pad(extended, ((0, 0), (0, 8), (0, 128)))
    device_id = lax.axis_index(("row", "col"))
    own_count = lax.dynamic_slice_in_dim(counts, device_id, 1)
    grad_ext, grad_probe, loss = compute(own_count, offsets[0].reshape(-1), extended, probe_field, patterns[0])
    from_above = shifted(grad_ext[:, tile : tile + pixels, : tile + pixels], "row", 1)
    upper = grad_ext[:, :tile, : tile + pixels].at[:, :pixels, :].add(from_above)
    from_left = shifted(upper[:, :, tile:], "col", 1)
    object_grad = upper[:, :, :tile].at[:, :, :pixels].add(from_left)
    probe_peak = jnp.max(jnp.sum(probe_field[0] * probe_field[0] + probe_field[1] * probe_field[1], axis=0))
    new_object = object_slab - object_grad / probe_peak
    local_peak = jnp.max(object_slab[0] * object_slab[0] + object_slab[1] * object_slab[1])
    largest = lax.pmax(local_peak, ("row", "col"))
    scans = jnp.sum(counts).astype(jnp.float32) * (pixels * pixels)
    probe_total, loss_total = lax.psum((grad_probe, 0.5 * jnp.sum(loss)), ("row", "col"))
    new_probe = probe_field - probe_total / largest
    return (new_object, new_probe, loss_total / scans)


def solution(mesh):
    placed = (
        P(None, "row", "col"),
        P(),
        P(("row", "col"), None, None, None),
        P(("row", "col"), None, None),
        P(),
    )
    return jax.shard_map(
        body,
        mesh=mesh,
        in_specs=placed,
        out_specs=(P(None, "row", "col"), P(), P()),
        check_vma=False,
    )
```

time: 524 us -> 294 us (0.56)
  starting transfers between devices: 140 us -> 17.8 us
  blocking collectives: 202 us -> 151 us
  matrix products: 44.6 us -> 0 us
  Pallas kernels: 0 us -> 16.4 us
  local copies, waits for them, and re-layouts: 27.7 us -> 13.7 us
  loops' own time: 11.6 us -> 0 us
    ppermute x4, starting transfers between devices: 140 us -> 17.8 us  [shifted(): return lax.ppermute(shard, axis, pairs)]
    pmax x1, blocking collectives: 137 us -> 86.7 us  [body(): largest = lax.pmax(local_peak, ('row', 'col'))]
    dot_general x16 -> x0, matrix products: 44.6 us -> none  [the longest x2 5.98 us: transform(): jnp.einsum('mkn,nj->mkj', left_im, table_re, precision=highest)]
    pallas_call x0 -> x1, Pallas kernels: none -> 16.4 us  [compute(): pl.pallas_call(compute_kernel, out_shape=(jax.ShapeDtypeStruct((2, 776, 8...]
    another operation x1 -> x0, loops' own time: 11.6 us -> none  [body(): lax.fori_loop(0, own_count, own_slot, start)]
    dynamic_update_slice x1 -> x0, local copies, waits for them, and re-layouts: 6.48 us -> none  [add_patch(): lax.dynamic_update_slice(grad_ext, current + gradient, (0, row_at, col_at))]
  transfers between devices with their start and end apart: 5 -> 5, of which waited for: 3 -> 3; matrix products, arithmetic and copies ran while one was open for 2% -> 6% of each run, Pallas kernels for 0% -> 0%
where the time goes in v1:
time: 294 us; the launch traced here: 293 us
  blocking collectives  151 us (51%)
  waiting for transfers between devices  59.6 us (20%)
  other arithmetic  18.2 us (6%)
  starting transfers between devices  17.8 us (6%)
  between operations  17.3 us (6%)
  Pallas kernels  16.4 us (6%)
  local copies, waits for them, and re-layouts  13.7 us (5%)
    pmax x1, blocking collectives, body(): largest = lax.pmax(local_peak, ('row', 'col'))  86.7 us
    psum x1, blocking collectives, body(): lax.psum((grad_probe, 0.5 * jnp.sum(loss)), ('row', 'col'))  63.8 us
    ppermute x4, waiting for transfers between devices, shifted(): return lax.ppermute(shard, axis, pairs)  59.6 us
    ppermute x4, starting transfers between devices, shifted(): return lax.ppermute(shard, axis, pairs)  17.8 us
    pallas_call x1, Pallas kernels, compute(): pl.pallas_call(compute_kernel, out_shape=(jax.ShapeDtypeStruct((2, 776, 8...  16.4 us
  transfers between devices with their start and end apart: 5, of which 3 were waited for; matrix products, arithmetic and copies ran while one was open for 6% of the time, Pallas kernels for 0%

profile of v1, /device:TPU:1, one launch (start us, length us, event | category | flops | bytes accessed | tf_op | source)
XLA Modules:
  0.0 293.5 jit_solution(4463825622341992205)
XLA Ops:
  7.2 1.4 slice.84
  8.7 1.3 collective-permute-start
  10.0 0.2 constant_dynamic-update-slice_fusion.1
  10.1 25.7 %collective-permute-done = f32[2,512,256]{2,1,0:T(8,128)S(1)} collective-permute-done((f32[2,512,256]{2,1,0:T(8,128)S(1)}, f32[2,512,256]{2,1,0:T(8,128)S(1)}, u32[]{:S(2)}, u32[]{:S(2)}) %collective-permute-start) | collective-permute-done | bytes 1048608 | tf_op jit(solution)/shard_map/ppermute | solution.py:154
  36.0 1.7 copy-done.3
  37.6 1.2 slice.96
  38.9 3.1 %collective-permute-start.1 = (f32[2,256,768]{2,1,0:T(8,128)}, f32[2,256,768]{2,1,0:T(8,128)}, u32[]{:S(2)}, u32[]{:S(2)}) collective-permute-start(f32[2,256,768]{2,1,0:T(8,128)} %slice.96), channel_id=1, source_target_pairs={{16,0},{32,16},{48,32},{64,48},{80,64},{96,80},{112,96},{17,1},{33... | collective-permute-start | bytes 4718600 | tf_op jit(solution)/shard_map/ppermute | solution.py:154
  42.1 0.1 copy.15
  42.1 0.6 reshape_squeeze.3.off_ref
  42.7 0.6 dynamic_slice.3.count_ref
  43.3 18.3 %collective-permute-done.1 = f32[2,256,768]{2,1,0:T(8,128)} collective-permute-done((f32[2,256,768]{2,1,0:T(8,128)}, f32[2,256,768]{2,1,0:T(8,128)}, u32[]{:S(2)}, u32[]{:S(2)}) %collective-permute-start.1) | collective-permute-done | bytes 1572896 | tf_op jit(solution)/shard_map/ppermute | solution.py:154
  61.6 4.2 %select_maximum_fusion.ext = f32[2,776,896]{2,1,0:T(8,128)} fusion(f32[2,256,768]{2,1,0:T(8,128)} %collective-permute-done.1, f32[2,512,768]{2,1,0:T(8,128)} %copy-done.3), kind=kLoop, calls=%fused_computation | loop fusion | flops 11124736 | bytes 10280960 | tf_op jit(solution)/shard_map/concatenate | solution.py:163
  65.9 16.4 %compute.1 = (f32[2,776,896]{2,1,0:T(8,128)}, f32[2,4,256,256]{3,2,1,0:T(8,128)}, f32[8,128]{1,0:T(8,128)}) custom-call(s32[1]{0:T(128)} %dynamic_slice.3.count_ref, s32[8]{0:T(128)} %reshape_squeeze.3.off_ref, f32[2,776,896]{2,1,0:T(8,128)} %select_maximum_fusion.ext, f32[2,4,256,256]{3,2,1,0:T(8,128)} %probe.1, f32[4,256,256]{2,1,0:T(8,128)} %bitcast.1, ...), custom_call_target="tpu_custom_call" | custom-call | tf_op jit(solution)/shard_map/compute/pallas_call | solution.py:136
  82.2 2.7 slice.88
  84.9 1.9 collective-permute-start.2
  86.8 2.1 slice.86
  89.0 15.5 %collective-permute-done.2 = f32[2,256,768]{2,1,0:T(8,128)} collective-permute-done((f32[2,256,768]{2,1,0:T(8,128)}, f32[2,256,768]{2,1,0:T(8,128)}, u32[]{:S(2)}, u32[]{:S(2)}) %collective-permute-start.2) | collective-permute-done | bytes 1572896 | tf_op jit(solution)/shard_map/ppermute | solution.py:154
  104.5 2.1 add_dynamic-update-slice_fusion
  106.6 1.7 copy-done.1
  108.2 1.0 slice.99
  109.3 11.4 %collective-permute-start.3 = (f32[2,512,256]{2,1,0:T(8,128)}, f32[2,512,256]{2,1,0:T(8,128)S(1)}, u32[]{:S(2)}, u32[]{:S(2)}) collective-permute-start(f32[2,512,256]{2,1,0:T(8,128)} %slice.99), channel_id=1, source_target_pairs={{0,1},{1,2},{2,3},{3,4},{4,5},{5,6},{6,7},{7,8},{8,9},{9,10},{10,1... | collective-permute-start | bytes 3145736 | tf_op jit(solution)/shard_map/ppermute | solution.py:154
  120.7 0.9 add_reduce_fusion
  121.6 86.7 %pmax.7 = f32[]{:T(128)} all-reduce(f32[]{:T(128)} %add_reduce_fusion), channel_id=1, replica_groups=mesh['row'=8,'col'=16] {'row','col'}, use_global_device_ids=true, to_apply=%region_4.5 | all-reduce | flops 1 | bytes 8 | tf_op jit(solution)/shard_map/pmax | solution.py:175
  208.3 0.6 reduce_sum.29
  209.6 1.7 add_reduce_fusion.1
  211.3 0.6 reduce_sum.28
  212.6 0.7 reduce_max.18
  213.3 63.8 %psum.15 = f32[]{:T(128)} all-reduce(f32[]{:T(128)S(6)} %mul_shard_map.3), channel_id=1, replica_groups=mesh['row'=8,'col'=16] {'row','col'}, use_global_device_ids=true, to_apply=%region_6.7 | all-reduce | flops 1 | bytes 8 | tf_op jit(solution)/shard_map/psum | solution.py:177
  277.8 4.8 %divide_subtract_fusion = f32[2,4,256,256]{3,2,1,0:T(8,128)} fusion(f32[2,4,256,256]{3,2,1,0:T(8,128)} %probe.1, f32[2,4,256,256]{3,2,1,0:T(8,128)} %all-reduce.3.cloned.1.call-done, f32[]{:T(128)} %pmax.7), kind=kLoop, calls=%fused_computation.3 | loop fusion | flops 1048576 | bytes 6291460 | tf_op jit(solution)/shard_map/sub | solution.py:178
  282.5 0.3 slice.97
  282.9 0.2 fusion
  283.1 2.4 divide_subtract_fusion.1
  (17 shorter events, 0.2 us)
Async XLA Ops:
  7.2 2.8 copy-start
  7.2 270.6 %all-reduce.3.cloned.1.call-start = ((), (), s32[]{:S(2)}) async-start(), calls=%async_computation | async-start | bytes 4194304 | tf_op jit(solution)/shard_map/psum | solution.py:177
  8.7 27.2 %collective-permute-start = (f32[2,512,256]{2,1,0:T(8,128)S(1)}, f32[2,512,256]{2,1,0:T(8,128)S(1)}, u32[]{:S(2)}, u32[]{:S(2)}) collective-permute-start(f32[2,512,256]{2,1,0:T(8,128)S(1)} %slice.84), channel_id=1, source_target_pairs={{1,0},{2,1},{3,2},{4,3},{5,4},{6,5},{7,6},{8,7},{9,8},{10,9},{11,1... | collective-permute-start | bytes 3145736 | tf_op jit(solution)/shard_map/ppermute | solution.py:154
  36.0 1.7 copy-start.3
  37.6 4.4 %copy-start.5 = (s32[1,4,2]{1,2,0:T(2,128)S(1)}, s32[1,4,2]{1,2,0:T(2,128)}, u32[]{:S(2)}) copy-start(s32[1,4,2]{1,2,0:T(2,128)} %param.17) | copy-start | bytes 100
  37.6 5.1 %copy-start.6 = (s32[128]{0:T(128)S(1)}, s32[128]{0:T(128)}, u32[]{:S(2)}) copy-start(s32[128]{0:T(128)} %param.18) | copy-start | bytes 1540
  38.9 22.7 %collective-permute-start.1 = (f32[2,256,768]{2,1,0:T(8,128)}, f32[2,256,768]{2,1,0:T(8,128)}, u32[]{:S(2)}, u32[]{:S(2)}) collective-permute-start(f32[2,256,768]{2,1,0:T(8,128)} %slice.96), channel_id=1, source_target_pairs={{16,0},{32,16},{48,32},{64,48},{80,64},{96,80},{112,96},{17,1},{33... | collective-permute-start | bytes 4718600 | tf_op jit(solution)/shard_map/ppermute | solution.py:154
  84.9 19.6 %collective-permute-start.2 = (f32[2,256,768]{2,1,0:T(8,128)}, f32[2,256,768]{2,1,0:T(8,128)}, u32[]{:S(2)}, u32[]{:S(2)}) collective-permute-start(f32[2,256,768]{2,1,0:T(8,128)} %slice.88), channel_id=1, source_target_pairs={{0,16},{16,32},{32,48},{48,64},{64,80},{80,96},{96,112},{1,17},{17... | collective-permute-start | bytes 4718600 | tf_op jit(solution)/shard_map/ppermute | solution.py:154
  106.5 1.7 copy-start.1
  109.3 102.1 %copy-start.4 = (f32[8,128]{1,0:T(8,128)S(1)}, f32[8,128]{1,0:T(8,128)}, u32[]{:S(2)}) copy-start(f32[8,128]{1,0:T(8,128)} %get-tuple-element.32) | copy-start | bytes 12292
  109.3 173.6 %collective-permute-start.3 = (f32[2,512,256]{2,1,0:T(8,128)}, f32[2,512,256]{2,1,0:T(8,128)S(1)}, u32[]{:S(2)}, u32[]{:S(2)}) collective-permute-start(f32[2,512,256]{2,1,0:T(8,128)} %slice.99), channel_id=1, source_target_pairs={{0,1},{1,2},{2,3},{3,4},{4,5},{5,6},{6,7},{7,8},{8,9},{9,10},{10,1... | collective-permute-start | bytes 3145736 | tf_op jit(solution)/shard_map/ppermute | solution.py:154
  277.8 4.8 %copy-start.2 = (f32[2,512,768]{2,1,0:T(8,128)S(1)}, f32[2,512,768]{2,1,0:T(8,128)}, u32[]{:S(2)}) copy-start(f32[2,512,768]{2,1,0:T(8,128)} %copy-done.1) | copy-start | bytes 9437188
Sparse Core Ops, SparseCore 0:
  87.0 183.5 all-reduce.2

commit v2 on v1

--- a/solution.py
+++ b/solution.py
@@ -11,6 +11,7 @@
 
 N = 256
 H = 128
+
 
 def split(x):
     hi = x.astype(jnp.bfloat16)
@@ -52,15 +53,35 @@
     hi, lo = split(x)
     return dot(jnp.concatenate([hi, lo, hi], axis=1), t)
 
-def compute_kernel(count_ref, off_ref, ext, probe, pat, left, leftT, right, rightT, perm,
-                   gext, pgrad, loss_ref, patch, psi, res, acc, swap):
+def compute_kernel(counts, offsets, obj, hr, hb, probe, patterns, left, leftT, right, rightT, perm,
+                   gext, pgrad, loss_ref, ext, patch, psi, res, acc, swap, local):
+    loads = [
+        pltpu.make_async_copy(obj, ext.at[:, 0 : 2 * N, 0 : 2 * N], local.at[0]),
+        pltpu.make_async_copy(hr, ext.at[:, 0 : 2 * N, 2 * N : 3 * N], local.at[1]),
+        pltpu.make_async_copy(hb, ext.at[:, 2 * N : 3 * N, 0 : 3 * N], local.at[2]),
+    ]
+    for load in loads:
+        load.start()
+    row = lax.axis_index("row")
+    col = lax.axis_index("col")
+    count = counts[row * 16 + col]
     gext[...] = jnp.zeros_like(gext)
     pgrad[...] = jnp.zeros_like(pgrad)
     loss_ref[...] = jnp.zeros_like(loss_ref)
+    for load in loads:
+        load.wait()
+
+    @pl.when(col == 15)
+    def _():
+        ext[:, :, 2 * N : 3 * N] = jnp.zeros((2, 776, N), jnp.float32)
+
+    @pl.when(row == 7)
+    def _():
+        ext[:, 2 * N : 3 * N, :] = jnp.zeros((2, N, 896), jnp.float32)
 
     def slot(s, _):
-        r = off_ref[2 * s]
-        c = off_ref[2 * s + 1]
+        r = offsets[0, s, 0]
+        c = offsets[0, s, 1]
         ca = pl.multiple_of(c // 128 * 128, 128)
         cs = c - ca
         ra = pl.multiple_of(r // 8 * 8, 8)
@@ -69,7 +90,7 @@
             x = ext[comp, pl.ds(ra, 264), pl.ds(ca, 384)]
             x = pltpu.roll(x, 384 - cs, 1)[:, :N]
             patch[comp] = pltpu.roll(x, 264 - rs, 0)[:N]
-        hi, lo = split(pat[s])
+        hi, lo = split(patterns[0, s])
         y = dot(hi, perm[...]) + dot(lo, perm[...])
         for q in (0, 1):
             swap[q] = y[:, q * H:(q + 1) * H]
@@ -127,56 +148,312 @@
             gext[comp, pl.ds(ra, 264), pl.ds(ca, 384)] += pltpu.roll(x, cs, 1)
         return 0
 
-    lax.fori_loop(0, count_ref[0], slot, 0)
-
-def compute(count, offs, ext, probe, pat):
-    left, leftT, right, rightT, perm = [jnp.asarray(t) for t in tables()]
+    lax.fori_loop(0, count, slot, 0)
+    scans = lax.fori_loop(0, counts.shape[0], lambda i, t: t + counts[i], 0)
+    loss_ref[...] = loss_ref[...] * (0.5 / (scans.astype(jnp.float32) * (N * N)))
+
+    @pl.when(col == 15)
+    def _():
+        gext[:, :, 2 * N : 3 * N] = jnp.zeros((2, 776, N), jnp.float32)
+
+    @pl.when(row == 7)
+    def _():
+        gext[:, 2 * N : 3 * N, :] = jnp.zeros((2, N, 896), jnp.float32)
+
+
+def compute(counts, offsets, obj, hr, hb, probe, patterns):
+    consts = [jnp.asarray(t) for t in tables()]
     V = pl.BlockSpec(memory_space=pltpu.VMEM)
     S = pl.BlockSpec(memory_space=pltpu.SMEM)
+    A = pl.BlockSpec(memory_space=pl.ANY)
     return pl.pallas_call(
         compute_kernel,
-        out_shape=(jax.ShapeDtypeStruct((2, 776, 896), jnp.float32),
-                   jax.ShapeDtypeStruct((2, 4, N, N), jnp.float32),
-                   jax.ShapeDtypeStruct((8, 128), jnp.float32)),
-        in_specs=[S, S] + [V] * 8,
+        out_shape=(
+            jax.ShapeDtypeStruct((2, 776, 896), jnp.float32),
+            jax.ShapeDtypeStruct((2, 4, N, N), jnp.float32),
+            jax.ShapeDtypeStruct((8, 128), jnp.float32),
+        ),
+        in_specs=[S, S] + [A] * 3 + [V] * 7,
         out_specs=(V, V, V),
-        scratch_shapes=[pltpu.VMEM((2, N, N), jnp.float32), pltpu.VMEM((4, 2, N, N), jnp.float32),
-                        pltpu.VMEM((2, N, H), jnp.float32), pltpu.VMEM((2, 264, 384), jnp.float32),
-                        pltpu.VMEM((2, N, H), jnp.float32)],
+        scratch_shapes=[
+            pltpu.VMEM((2, 776, 896), jnp.float32),
+            pltpu.VMEM((2, N, N), jnp.float32),
+            pltpu.VMEM((4, 2, N, N), jnp.float32),
+            pltpu.VMEM((2, N, H), jnp.float32),
+            pltpu.VMEM((2, 264, 384), jnp.float32),
+            pltpu.VMEM((2, N, H), jnp.float32),
+            pltpu.SemaphoreType.DMA((3,)),
+        ],
         compiler_params=pltpu.CompilerParams(vmem_limit_bytes=56 << 20),
         name="compute",
-    )(count, offs, ext, probe, pat, left, leftT, right, rightT, perm)
-
-
-def shifted(shard, axis, by):
-    size = lax.axis_size(axis)
-    pairs = [(i, i + by) for i in range(size) if 0 <= i + by < size]
-    return lax.ppermute(shard, axis, pairs)
+    )(counts, offsets, obj, hr, hb, probe, patterns, *consts)
+
+
+MESH = pl.DeviceIdType.MESH
+F32 = jnp.float32
+
+
+def place():
+    row = lax.axis_index("row")
+    col = lax.axis_index("col")
+    return col // 4, row // 2, col % 4, row % 2
+
+
+def device_at(x, y, z, k):
+    return (lax.rem(y + 8, 4) * 2 + k, lax.rem(x + 8, 4) * 4 + lax.rem(z + 8, 4))
+
+
+def neighbours():
+    row = lax.axis_index("row")
+    col = lax.axis_index("col")
+    left = (row, lax.rem(col + 15, 16))
+    right = (row, lax.rem(col + 1, 16))
+    above = (lax.rem(row + 7, 8), col)
+    below = (lax.rem(row + 1, 8), col)
+    return left, right, above, below
+
+
+def groups():
+    x, y, z, k = place()
+    return {
+        "k": [device_at(x, y, z, 1 - k)],
+        "x": [device_at(x + d, y, z, k) for d in (1, 2, 3)],
+        "y": [device_at(x, y + d, z, k) for d in (1, 2, 3)],
+        "z": [device_at(x, y, z + d, k) for d in (1, 2, 3)],
+    }
+
+
+def greet():
+    peers = list(neighbours())
+    for axis in ("k", "x", "y", "z"):
+        peers += groups()[axis]
+    barrier = pltpu.get_barrier_semaphore()
+    for peer in peers:
+        pl.semaphore_signal(barrier, inc=1, device_id=peer, device_id_type=MESH)
+    pl.semaphore_wait(barrier, len(peers))
+
+
+def remote(src, dst, send, recv, i, peer):
+    copy = pltpu.make_async_remote_copy(
+        src_ref=src, dst_ref=dst, send_sem=send.at[i], recv_sem=recv.at[i], device_id=peer, device_id_type=MESH
+    )
+    copy.start()
+    return copy
+
+
+class Small:
+    def __init__(self, op, value, slots, send, recv, base):
+        self.op, self.value, self.slots, self.send, self.recv, self.base = op, value, slots, send, recv, base
+        self.step, self.at = 0, 0
+
+    def start(self):
+        peers = groups()["kxyz"[self.step]]
+        self.copies = []
+        for peer in peers:
+            self.copies.append(
+                remote(self.value.at[self.step], self.slots.at[self.at], self.send, self.recv, self.base + self.at, peer)
+            )
+            self.at += 1
+
+    def finish(self):
+        total = self.value[self.step]
+        first = self.at - len(self.copies)
+        for i, copy in enumerate(self.copies):
+            copy.wait()
+            total = self.op(total, self.slots[first + i])
+        self.step += 1
+        self.value[self.step] = total
+
+
+def halo_kernel(obj, hr, hb, peak, mine, value, slots, local, send, recv):
+    own = pltpu.make_async_copy(obj, mine, local.at[0])
+    own.start()
+    left, right, above, below = neighbours()
+    greet()
+    n = 256
+    top = remote(obj.at[:, 0:n, 0:n], hr.at[:, 0:n, :], send, recv, 0, left)
+    side = remote(obj.at[:, 0:n, :], hb.at[:, :, 0 : 2 * n], send, recv, 2, above)
+    bottom = remote(obj.at[:, n : 2 * n, 0:n], hr.at[:, n : 2 * n, :], send, recv, 1, left)
+    own.wait()
+
+    def largest(i, best):
+        re = mine[0, pl.ds(pl.multiple_of(i * 16, 16), 16), :]
+        im = mine[1, pl.ds(pl.multiple_of(i * 16, 16), 16), :]
+        return jnp.maximum(best, re * re + im * im)
+
+    best = lax.fori_loop(0, 32, largest, jnp.zeros((16, 512), F32))
+    value[0] = jnp.full((8, 128), jnp.max(best), F32)
+    peaks = Small(jnp.maximum, value, slots, send, recv, 4)
+    for _ in range(4):
+        peaks.start()
+        peaks.finish()
+    peak[...] = value[4]
+    top.wait_recv()
+    corner = remote(hr.at[:, 0:n, :], hb.at[:, :, 2 * n : 3 * n], send, recv, 3, above)
+    top.wait_send()
+    side.wait()
+    corner.wait()
+    bottom.wait()
+
+
+def halo(obj):
+    V = pl.BlockSpec(memory_space=pltpu.VMEM)
+    A = pl.BlockSpec(memory_space=pl.ANY)
+    return pl.pallas_call(
+        halo_kernel,
+        out_shape=(
+            jax.ShapeDtypeStruct((2, 512, 256), F32),
+            jax.ShapeDtypeStruct((2, 256, 768), F32),
+            jax.ShapeDtypeStruct((8, 128), F32),
+        ),
+        in_specs=[A],
+        out_specs=(A, A, V),
+        scratch_shapes=[
+            pltpu.VMEM((2, 512, 512), F32),
+            pltpu.VMEM((5, 8, 128), F32),
+            pltpu.VMEM((10, 8, 128), F32),
+            pltpu.SemaphoreType.DMA((1,)),
+            pltpu.SemaphoreType.DMA((14,)),
+            pltpu.SemaphoreType.DMA((14,)),
+        ],
+        compiler_params=pltpu.CompilerParams(collective_id=0, has_side_effects=True, vmem_limit_bytes=32 << 20),
+        name="halo",
+    )(obj)
+
+
+def shares(axis, rows):
+    x, y, z, k = place()
+    mine = {"k": k, "x": x, "y": y, "z": z}[axis]
+    size = 2 if axis == "k" else 4
+    part = rows // size
+    others = [(lax.rem(mine + d, size) * part) for d in range(1, size)]
+    return mine * part, others, part
+
+
+def exchange_kernel(gext, pg, obj, probe, peak, loss, new_obj, new_probe, loss_mean,
+                    own, tile, field, total, corner, strip, over, side,
+                    r0, rx, ry, rz, value, slots, local, send, recv):
+    n = 256
+    left, right, above, below = neighbours()
+    loads = [
+        pltpu.make_async_copy(pg, total, local.at[0]),
+        pltpu.make_async_copy(gext.at[:, 0:n, 2 * n : 3 * n], strip, local.at[1]),
+        pltpu.make_async_copy(gext.at[:, 0 : 2 * n, 0 : 2 * n], own, local.at[2]),
+        pltpu.make_async_copy(obj, tile, local.at[3]),
+        pltpu.make_async_copy(probe, field, local.at[4]),
+    ]
+    for load in loads:
+        load.start()
+    greet()
+    t1 = remote(gext.at[:, 2 * n : 3 * n, 2 * n : 3 * n], corner, send, recv, 0, below)
+    t2 = remote(gext.at[:, n : 2 * n, 2 * n : 3 * n], side.at[:, n : 2 * n, :], send, recv, 1, right)
+    t3 = remote(gext.at[:, 2 * n : 3 * n, 0 : 2 * n], over, send, recv, 2, below)
+    value[0] = loss[...]
+    misfit = Small(jnp.add, value, slots, send, recv, 4)
+    misfit.start()
+    group = groups()
+    at = 14
+    base, rows = 0, 2048
+    trail = []
+    pending = []
+    for axis, got in (("k", r0), ("x", rx), ("y", ry), ("z", rz)):
+        mine, others, part = shares(axis, rows)
+        copies = []
+        source = pg if axis == "k" else total
+        for i, (peer, other) in enumerate(zip(group[axis], others)):
+            copies.append(remote(source.at[pl.ds(pl.multiple_of(base + other, 16), part), :], got.at[i], send, recv, at, peer))
+            at += 1
+        if axis == "k":
+            for load in loads:
+                load.wait()
+        misfit.finish()
+        if axis != "z":
+            misfit.start()
+        if axis == "x":
+            t1.wait_recv()
+            strip[...] += corner[...]
+            t4 = remote(strip, side.at[:, 0:n, :], send, recv, 3, right)
+        keep = pl.ds(pl.multiple_of(base + mine, 16), part)
+        for i, copy in enumerate(copies):
+            copy.wait_recv()
+        pending += copies
+        sums = total[keep, :]
+        for i in range(len(copies)):
+            sums += got[i]
+        total[keep, :] = sums
+        trail.append((axis, base, rows, keep))
+        base, rows = base + mine, part
+    loss_mean[0, 0] = jnp.sum(value[4])
+    keep = pl.ds(pl.multiple_of(base, 16), rows)
+    scale = 1.0 / peak[0:1, 0:1]
+    new_probe[keep, :] = field[keep, :] - total[keep, :] * scale
+    for axis, base, rows, keep in reversed(trail):
+        whole = pl.ds(pl.multiple_of(base, 16), rows)
+        mine, others, part = shares(axis, rows)
+        copies = []
+        for peer in group[axis]:
+            copies.append(remote(new_probe.at[keep, :], new_probe.at[keep, :], send, recv, at, peer))
+            at += 1
+        for copy in copies:
+            copy.wait_recv()
+        pending += copies
+    probe_peak = jnp.max(
+        sum(field[m * n : (m + 1) * n, :] * field[m * n : (m + 1) * n, :] for m in range(8))
+    )
+    inverse = 1.0 / probe_peak
+    t3.wait_recv()
+    own[:, 0:n, :] += over[...]
+    new_obj[:, :, n : 2 * n] = tile[:, :, n : 2 * n] - own[:, :, n : 2 * n] * inverse
+    t2.wait_recv()
+    t4.wait_recv()
+    new_obj[:, :, 0:n] = tile[:, :, 0:n] - (own[:, :, 0:n] + side[...]) * inverse
+    for copy in pending + [t1, t2, t3, t4]:
+        copy.wait_send()
+
+
+def exchange(gext, pg, obj, probe, peak, loss):
+    V = pl.BlockSpec(memory_space=pltpu.VMEM)
+    A = pl.BlockSpec(memory_space=pl.ANY)
+    S = pl.BlockSpec(memory_space=pltpu.SMEM)
+    copies = 14 + 2 * 10
+    new_obj, new_probe, loss_mean = pl.pallas_call(
+        exchange_kernel,
+        out_shape=(
+            jax.ShapeDtypeStruct((2, 512, 512), F32),
+            jax.ShapeDtypeStruct((2048, 256), F32),
+            jax.ShapeDtypeStruct((1, 1), F32),
+        ),
+        in_specs=[A, A, A, A, V, V],
+        out_specs=(V, V, S),
+        scratch_shapes=[
+            pltpu.VMEM((2, 512, 512), F32),
+            pltpu.VMEM((2, 512, 512), F32),
+            pltpu.VMEM((2048, 256), F32),
+            pltpu.VMEM((2048, 256), F32),
+            pltpu.VMEM((2, 256, 256), F32),
+            pltpu.VMEM((2, 256, 256), F32),
+            pltpu.VMEM((2, 256, 512), F32),
+            pltpu.VMEM((2, 512, 256), F32),
+            pltpu.VMEM((1, 1024, 256), F32),
+            pltpu.VMEM((3, 256, 256), F32),
+            pltpu.VMEM((3, 64, 256), F32),
+            pltpu.VMEM((3, 16, 256), F32),
+            pltpu.VMEM((5, 8, 128), F32),
+            pltpu.VMEM((10, 8, 128), F32),
+            pltpu.SemaphoreType.DMA((5,)),
+            pltpu.SemaphoreType.DMA((copies,)),
+            pltpu.SemaphoreType.DMA((copies,)),
+        ],
+        compiler_params=pltpu.CompilerParams(collective_id=1, has_side_effects=True, vmem_limit_bytes=48 << 20),
+        name="exchange",
+    )(gext, pg.reshape(2048, 256), obj, probe.reshape(2048, 256), peak, loss)
+    return new_obj, new_probe.reshape(probe.shape), loss_mean.reshape(())
 
 
 def body(object_slab, probe_field, patterns, offsets, counts):
-    tile = object_slab.shape[1]
-    pixels = probe_field.shape[2]
-    from_right = shifted(object_slab[:, :, :pixels], "col", -1)
-    widened = jnp.concatenate([object_slab, from_right], axis=2)
-    from_below = shifted(widened[:, :pixels, :], "row", -1)
-    extended = jnp.concatenate([widened, from_below], axis=1)
-    extended = jnp.pad(extended, ((0, 0), (0, 8), (0, 128)))
-    device_id = lax.axis_index(("row", "col"))
-    own_count = lax.dynamic_slice_in_dim(counts, device_id, 1)
-    grad_ext, grad_probe, loss = compute(own_count, offsets[0].reshape(-1), extended, probe_field, patterns[0])
-    from_above = shifted(grad_ext[:, tile : tile + pixels, : tile + pixels], "row", 1)
-    upper = grad_ext[:, :tile, : tile + pixels].at[:, :pixels, :].add(from_above)
-    from_left = shifted(upper[:, :, tile:], "col", 1)
-    object_grad = upper[:, :, :tile].at[:, :, :pixels].add(from_left)
-    probe_peak = jnp.max(jnp.sum(probe_field[0] * probe_field[0] + probe_field[1] * probe_field[1], axis=0))
-    new_object = object_slab - object_grad / probe_peak
-    local_peak = jnp.max(object_slab[0] * object_slab[0] + object_slab[1] * object_slab[1])
-    largest = lax.pmax(local_peak, ("row", "col"))
-    scans = jnp.sum(counts).astype(jnp.float32) * (pixels * pixels)
-    probe_total, loss_total = lax.psum((grad_probe, 0.5 * jnp.sum(loss)), ("row", "col"))
-    new_probe = probe_field - probe_total / largest
-    return (new_object, new_probe, loss_total / scans)
+    hr, hb, peak = halo(object_slab)
+    gext, pg, loss = compute(counts, offsets, object_slab, hr, hb, probe_field, patterns)
+    return exchange(gext, pg, object_slab, probe_field, peak, loss)
 
 
 def solution(mesh):

time: 294 us -> 154 us (0.52)
  blocking collectives: 151 us -> 0 us
  Pallas kernels: 16.4 us -> 143 us
  waiting for transfers between devices: 59.6 us -> 0 us
  other arithmetic: 18.2 us -> 0 us
  starting transfers between devices: 17.8 us -> 0 us
  between operations: 17.3 us -> 2.38 us
  local copies, waits for them, and re-layouts: 13.7 us -> 8.35 us
    pallas_call x0 -> x2, Pallas kernels: none -> 119 us  [the longest x1 74.4 us: exchange(): pl.pallas_call(exchange_kernel, out_shape=(jax.ShapeDtypeStruct((2, 512,...]
    pmax x1 -> x0, blocking collectives: 86.7 us -> none  [body(): largest = lax.pmax(local_peak, ('row', 'col'))]
    psum x1 -> x0, blocking collectives: 63.8 us -> none  [body(): lax.psum((grad_probe, 0.5 * jnp.sum(loss)), ('row', 'col'))]
    ppermute x4 -> x0, waiting for transfers between devices: 59.6 us -> none  [shifted(): return lax.ppermute(shard, axis, pairs)]
    ppermute x4 -> x0, starting transfers between devices: 17.8 us -> none  [shifted(): return lax.ppermute(shard, axis, pairs)]
    slice x6 -> x0, local copies, waits for them, and re-layouts: 8.8 us -> none  [the longest x1 2.66 us: body(): grad_ext[:, tile:tile + pixels, :tile + pixels]]
    pallas_call x1, Pallas kernels: 16.4 us -> 24.7 us  [compute(): pl.pallas_call(compute_kernel, out_shape=(jax.ShapeDtypeStruct((2, 776, 8...]
    sub x2 -> x0, other arithmetic: 7.2 us -> none  [the longest x1 4.75 us: body(): new_probe = probe_field - probe_total / largest]
  transfers between devices with their start and end apart: 5 -> 0, of which waited for: 3 -> 0; matrix products, arithmetic and copies ran while one was open for 6% -> 0% of each run, Pallas kernels for 0% -> 0%
where the time goes in v2:
time: 154 us
  Pallas kernels  143 us (93%)
  local copies, waits for them, and re-layouts  8.35 us (5%)
  between operations  2.38 us (2%)
    pallas_call x1, Pallas kernels, exchange(): pl.pallas_call(exchange_kernel, out_shape=(jax.ShapeDtypeStruct((2, 512,...  74.4 us
    pallas_call x1, Pallas kernels, halo(): pl.pallas_call(halo_kernel, out_shape=(jax.ShapeDtypeStruct((2, 512, 256)...  44.1 us
    pallas_call x1, Pallas kernels, compute(): pl.pallas_call(compute_kernel, out_shape=(jax.ShapeDtypeStruct((2, 776, 8...  24.7 us
    unnamed x11, local copies, waits for them, and re-layouts  8.35 us

profile of v2, /device:TPU:1, one launch (start us, length us, event | category | flops | bytes accessed | tf_op | source)
XLA Modules:
  0.0 153.9 jit_solution(4499191167492457736)
XLA Ops:
  0.6 1.3 copy.13.offsets
  2.0 0.0 copy-start
  2.0 1.6 %copy-done = f32[2,512,512]{2,1,0:T(8,128)S(1)} copy-done((f32[2,512,512]{2,1,0:T(8,128)S(1)}, f32[2,512,512]{2,1,0:T(8,128)}, u32[]{:S(2)}) %copy-start) | copy-done | bytes 2097176
  3.6 44.1 %halo.1 = (f32[2,512,256]{2,1,0:T(8,128)S(1)}, f32[2,256,768]{2,1,0:T(8,128)S(1)}, f32[8,128]{1,0:T(8,128)S(1)}) custom-call(f32[2,512,512]{2,1,0:T(8,128)S(1)} %copy-done), custom_call_target="tpu_custom_call" | custom-call | tf_op jit(solution)/shard_map/halo/pallas_call | solution.py:302
  47.7 0.0 copy-start.1
  47.7 1.1 copy-done.1
  48.8 0.0 copy-start.2
  48.8 1.0 copy-done.2
  49.8 24.7 %compute.1 = (f32[2,776,896]{2,1,0:T(8,128)}, f32[2,4,256,256]{3,2,1,0:T(8,128)}, f32[8,128]{1,0:T(8,128)}) custom-call(s32[128]{0:T(128)} %counts.1, s32[1,4,2]{2,1,0:T(4,128)} %copy.13.offsets, f32[2,512,512]{2,1,0:T(8,128)} %obj.5, f32[2,512,256]{2,1,0:T(8,128)} %copy-done.2, f32[2,256,768]{2,1,0:T(8,128)} %copy-done.1, f32[2,4,256,256]{3,2,1,0:T(8,128)} %probe.1, ...), custom_call_target="tpu_custom_call" | custom-call | tf_op jit(solution)/shard_map/compute/pallas_call | solution.py:169
  74.5 0.0 copy-start.3
  74.5 0.7 copy-done.3
  75.2 74.4 %exchange.1 = (f32[2,512,512]{2,1,0:T(8,128)S(1)}, f32[2048,256]{1,0:T(8,128)S(1)}, f32[1,1]{1,0:T(1,128)}) custom-call(f32[2,776,896]{2,1,0:T(8,128)} %get-tuple-element.14.gext, f32[2048,256]{1,0:T(8,128)} %bitcast.6, f32[2,512,512]{2,1,0:T(8,128)} %obj.5, f32[2048,256]{1,0:T(8,128)} %bitcast.5, f32[8,128]{1,0:T(8,128)S(1)} %get-tuple-element.16.peak, ...), custom_call_target="tpu_custom_call" | custom-call | tf_op jit(solution)/shard_map/exchange/pallas_call | solution.py:419
  149.6 1.3 copy.17
  150.9 1.3 copy.18
Async XLA Ops:
  2.0 1.6 %copy-start = (f32[2,512,512]{2,1,0:T(8,128)S(1)}, f32[2,512,512]{2,1,0:T(8,128)}, u32[]{:S(2)}) copy-start(f32[2,512,512]{2,1,0:T(8,128)} %obj.5) | copy-start | bytes 6291460
  47.7 1.1 copy-start.1
  48.8 1.0 copy-start.2
  74.5 0.7 copy-start.3

commit v3 on v2

--- a/solution.py
+++ b/solution.py
@@ -114,7 +114,7 @@
                 psi[m, q] = x
                 res[q] += x[:, :H] * x[:, :H] + x[:, H:] * x[:, H:]
             return 0
-        lax.fori_loop(0, 4, fwd, 0)
+        lax.fori_loop(0, 4, fwd, 0, unroll=True)
         loss_ref[...] += jnp.sum((res[0] * res[0] + res[1] * res[1]).reshape(32, 8, 128), axis=0)
         acc[...] = jnp.zeros_like(acc)
 
@@ -142,7 +142,7 @@
                 pgrad[0, m, sl] += orr * br + oi * bi
                 pgrad[1, m, sl] += orr * bi - oi * br
             return 0
-        lax.fori_loop(0, 4, bwd, 0)
+        lax.fori_loop(0, 4, bwd, 0, unroll=True)
         for comp in (0, 1):
             x = pltpu.roll(acc[comp], rs, 0)
             gext[comp, pl.ds(ra, 264), pl.ds(ca, 384)] += pltpu.roll(x, cs, 1)
@@ -184,7 +184,7 @@
             pltpu.VMEM((2, N, H), jnp.float32),
             pltpu.SemaphoreType.DMA((3,)),
         ],
-        compiler_params=pltpu.CompilerParams(vmem_limit_bytes=56 << 20),
+        compiler_params=pltpu.CompilerParams(vmem_limit_bytes=24 << 20),
         name="compute",
     )(counts, offsets, obj, hr, hb, probe, patterns, *consts)
 
@@ -223,10 +223,7 @@
     }
 
 
-def greet():
-    peers = list(neighbours())
-    for axis in ("k", "x", "y", "z"):
-        peers += groups()[axis]
+def greet(peers):
     barrier = pltpu.get_barrier_semaphore()
     for peer in peers:
         pl.semaphore_signal(barrier, inc=1, device_id=peer, device_id_type=MESH)
@@ -245,31 +242,38 @@
     def __init__(self, op, value, slots, send, recv, base):
         self.op, self.value, self.slots, self.send, self.recv, self.base = op, value, slots, send, recv, base
         self.step, self.at = 0, 0
+        self.done = []
 
     def start(self):
-        peers = groups()["kxyz"[self.step]]
+        axis = "kxyz"[self.step]
+        mine = dict(zip("xyzk", place()))[axis]
+        self.slots[self.step, mine] = self.value[self.step]
         self.copies = []
-        for peer in peers:
+        for peer in groups()[axis]:
             self.copies.append(
-                remote(self.value.at[self.step], self.slots.at[self.at], self.send, self.recv, self.base + self.at, peer)
+                remote(
+                    self.value.at[self.step], self.slots.at[self.step, mine], self.send, self.recv,
+                    self.base + self.at, peer,
+                )
             )
             self.at += 1
 
     def finish(self):
-        total = self.value[self.step]
-        first = self.at - len(self.copies)
-        for i, copy in enumerate(self.copies):
-            copy.wait()
-            total = self.op(total, self.slots[first + i])
+        for copy in self.copies:
+            copy.wait_recv()
+        self.done += self.copies
+        total = self.slots[self.step, 0]
+        for i in range(1, len(self.copies) + 1):
+            total = self.op(total, self.slots[self.step, i])
         self.step += 1
         self.value[self.step] = total
 
 
-def halo_kernel(obj, hr, hb, peak, mine, value, slots, local, send, recv):
+def halo_kernel(obj, hr, hb, peak, mine, local, send, recv):
     own = pltpu.make_async_copy(obj, mine, local.at[0])
     own.start()
     left, right, above, below = neighbours()
-    greet()
+    greet(list(neighbours()))
     n = 256
     top = remote(obj.at[:, 0:n, 0:n], hr.at[:, 0:n, :], send, recv, 0, left)
     side = remote(obj.at[:, 0:n, :], hb.at[:, :, 0 : 2 * n], send, recv, 2, above)
@@ -282,12 +286,7 @@
         return jnp.maximum(best, re * re + im * im)
 
     best = lax.fori_loop(0, 32, largest, jnp.zeros((16, 512), F32))
-    value[0] = jnp.full((8, 128), jnp.max(best), F32)
-    peaks = Small(jnp.maximum, value, slots, send, recv, 4)
-    for _ in range(4):
-        peaks.start()
-        peaks.finish()
-    peak[...] = value[4]
+    peak[...] = jnp.full((8, 128), jnp.max(best), F32)
     top.wait_recv()
     corner = remote(hr.at[:, 0:n, :], hb.at[:, :, 2 * n : 3 * n], send, recv, 3, above)
     top.wait_send()
@@ -306,116 +305,188 @@
             jax.ShapeDtypeStruct((2, 256, 768), F32),
             jax.ShapeDtypeStruct((8, 128), F32),
         ),
-        in_specs=[A],
+        in_specs=[pl.BlockSpec(memory_space=pltpu.HBM)],
         out_specs=(A, A, V),
         scratch_shapes=[
             pltpu.VMEM((2, 512, 512), F32),
-            pltpu.VMEM((5, 8, 128), F32),
-            pltpu.VMEM((10, 8, 128), F32),
             pltpu.SemaphoreType.DMA((1,)),
-            pltpu.SemaphoreType.DMA((14,)),
-            pltpu.SemaphoreType.DMA((14,)),
+            pltpu.SemaphoreType.DMA((4,)),
+            pltpu.SemaphoreType.DMA((4,)),
         ],
-        compiler_params=pltpu.CompilerParams(collective_id=0, has_side_effects=True, vmem_limit_bytes=32 << 20),
+        compiler_params=pltpu.CompilerParams(collective_id=0, has_side_effects=True, vmem_limit_bytes=6 << 20),
         name="halo",
     )(obj)
 
 
-def shares(axis, rows):
-    x, y, z, k = place()
-    mine = {"k": k, "x": x, "y": y, "z": z}[axis]
-    size = 2 if axis == "k" else 4
-    part = rows // size
-    others = [(lax.rem(mine + d, size) * part) for d in range(1, size)]
-    return mine * part, others, part
+PARTS = ((0, 384, "xyz"), (384, 384, "yzx"), (768, 256, "zxy"))
 
 
 def exchange_kernel(gext, pg, obj, probe, peak, loss, new_obj, new_probe, loss_mean,
-                    own, tile, field, total, corner, strip, over, side,
-                    r0, rx, ry, rz, value, slots, local, send, recv):
+                    strip, corner, over, side, r0, r1, r2, rz, value, slots, send, recv):
     n = 256
     left, right, above, below = neighbours()
-    loads = [
-        pltpu.make_async_copy(pg, total, local.at[0]),
-        pltpu.make_async_copy(gext.at[:, 0:n, 2 * n : 3 * n], strip, local.at[1]),
-        pltpu.make_async_copy(gext.at[:, 0 : 2 * n, 0 : 2 * n], own, local.at[2]),
-        pltpu.make_async_copy(obj, tile, local.at[3]),
-        pltpu.make_async_copy(probe, field, local.at[4]),
-    ]
-    for load in loads:
-        load.start()
-    greet()
-    t1 = remote(gext.at[:, 2 * n : 3 * n, 2 * n : 3 * n], corner, send, recv, 0, below)
-    t2 = remote(gext.at[:, n : 2 * n, 2 * n : 3 * n], side.at[:, n : 2 * n, :], send, recv, 1, right)
-    t3 = remote(gext.at[:, 2 * n : 3 * n, 0 : 2 * n], over, send, recv, 2, below)
-    value[0] = loss[...]
-    misfit = Small(jnp.add, value, slots, send, recv, 4)
-    misfit.start()
     group = groups()
-    at = 14
-    base, rows = 0, 2048
-    trail = []
-    pending = []
-    for axis, got in (("k", r0), ("x", rx), ("y", ry), ("z", rz)):
-        mine, others, part = shares(axis, rows)
+    x, y, z, k = place()
+    index = {"x": x, "y": y, "z": z, "k": k}
+    counter = [0]
+
+    def push(src, dst, peer):
+        counter[0] += 1
+        return remote(src, dst, send, recv, counter[0] - 1, peer)
+
+    def rows(start, size):
+        return pl.ds(pl.multiple_of(start, 8), size)
+
+    def op(a, b):
+        first = lax.broadcasted_iota(jnp.int32, (16, 128), 0) < 8
+        return jnp.where(first, a + b, jnp.maximum(a, b))
+
+    everyone = [group[a][i] for a in "kxyz" for i in range(len(group[a]))] + [left, right, above, below]
+    greet(everyone)
+    sent = []
+    over_sent, side_sent, corner_sent = [], [], []
+
+    def push_corner(i):
+        m = pl.ds(2 * n + 128 * i, 128)
+        corner_sent.append(push(gext.at[:, m, 2 * n : 3 * n], corner.at[:, 128 * i : 128 * i + 128], below))
+
+    def push_over(i):
+        m = pl.ds(2 * n + 64 * i, 64)
+        over_sent.append(push(gext.at[:, m, 0 : 2 * n], over.at[:, 64 * i : 64 * i + 64], below))
+
+    def push_side(i):
+        if i < 4:
+            m = pl.ds(n + 64 * i, 64)
+            side_sent.append(push(gext.at[:, m, 2 * n : 3 * n], side.at[:, m], right))
+        else:
+            m = pl.ds(64 * i - n, 64)
+            side_sent.append(push(strip.at[:, m], side.at[:, m], right))
+
+    def fold_corner(i):
+        corner_sent[i].wait_recv()
+        m = pl.ds(128 * i, 128)
+        strip[:, m] = gext[:, m, 2 * n : 3 * n] + corner[:, m]
+
+    swap = []
+    for first, size, _ in PARTS:
+        swap.append(push(pg.at[rows((1 - k) * 1024 + first, size)], r0.at[first : first + size], group["k"][0]))
+    push_corner(0)
+    push_side(0)
+    value[0, 0:8] = loss[...]
+    value[0, 8:16] = peak[...]
+    small = Small(op, value, slots, send, recv, 84)
+    small.start()
+
+    steps = []
+    for p, (first, size, axes) in enumerate(PARTS):
+        swap[p].wait_recv()
+        r0[first : first + size] += pg[rows(k * 1024 + first, size)]
+        q = size // 4
+        a = axes[0]
         copies = []
-        source = pg if axis == "k" else total
-        for i, (peer, other) in enumerate(zip(group[axis], others)):
-            copies.append(remote(source.at[pl.ds(pl.multiple_of(base + other, 16), part), :], got.at[i], send, recv, at, peer))
-            at += 1
-        if axis == "k":
-            for load in loads:
-                load.wait()
-        misfit.finish()
-        if axis != "z":
-            misfit.start()
-        if axis == "x":
-            t1.wait_recv()
-            strip[...] += corner[...]
-            t4 = remote(strip, side.at[:, 0:n, :], send, recv, 3, right)
-        keep = pl.ds(pl.multiple_of(base + mine, 16), part)
-        for i, copy in enumerate(copies):
+        for d, peer in enumerate(group[a]):
+            other = lax.rem(index[a] + d + 1, 4)
+            copies.append(push(r0.at[rows(first + other * q, q)], r1.at[d, first // 4 : first // 4 + q], peer))
+        steps.append(copies)
+    small.finish()
+    small.start()
+    push_corner(1)
+    push_side(1)
+    second = []
+    for p, (first, size, axes) in enumerate(PARTS):
+        q, e = size // 4, size // 16
+        a, b, c = axes
+        f1, f2 = first // 4, first // 16
+        for copy in steps[p]:
             copy.wait_recv()
-        pending += copies
-        sums = total[keep, :]
-        for i in range(len(copies)):
-            sums += got[i]
-        total[keep, :] = sums
-        trail.append((axis, base, rows, keep))
-        base, rows = base + mine, part
-    loss_mean[0, 0] = jnp.sum(value[4])
-    keep = pl.ds(pl.multiple_of(base, 16), rows)
-    scale = 1.0 / peak[0:1, 0:1]
-    new_probe[keep, :] = field[keep, :] - total[keep, :] * scale
-    for axis, base, rows, keep in reversed(trail):
-        whole = pl.ds(pl.multiple_of(base, 16), rows)
-        mine, others, part = shares(axis, rows)
+        sent += steps[p]
+        mine = rows(first + index[a] * q, q)
+        r0[mine] += r1[0, f1 : f1 + q] + r1[1, f1 : f1 + q] + r1[2, f1 : f1 + q]
         copies = []
-        for peer in group[axis]:
-            copies.append(remote(new_probe.at[keep, :], new_probe.at[keep, :], send, recv, at, peer))
-            at += 1
-        for copy in copies:
+        for d, peer in enumerate(group[b]):
+            other = lax.rem(index[b] + d + 1, 4)
+            copies.append(push(r0.at[rows(first + index[a] * q + other * e, e)], r2.at[d, f2 : f2 + e], peer))
+        second.append(copies)
+    small.finish()
+    small.start()
+    push_over(0)
+    push_side(2)
+    third = []
+    for p, (first, size, axes) in enumerate(PARTS):
+        q, e = size // 4, size // 16
+        a, b, c = axes
+        f2 = first // 16
+        for copy in second[p]:
             copy.wait_recv()
-        pending += copies
-    probe_peak = jnp.max(
-        sum(field[m * n : (m + 1) * n, :] * field[m * n : (m + 1) * n, :] for m in range(8))
-    )
+        sent += second[p]
+        mine = rows(first + index[a] * q + index[b] * e, e)
+        total = r0[mine] + r2[0, f2 : f2 + e] + r2[1, f2 : f2 + e] + r2[2, f2 : f2 + e]
+        r0[mine] = total
+        rz[index[c], f2 : f2 + e] = total
+        third.append([push(r0.at[mine], rz.at[index[c], f2 : f2 + e], peer) for peer in group[c]])
+    small.finish()
+    small.start()
+    push_over(1)
+    push_side(3)
+    fold_corner(0)
+    fold_corner(1)
+    small.finish()
+    loss_mean[0, 0] = jnp.sum(value[4, 0:8])
+    scale = 1.0 / value[4, 8:9, 0:1]
+
+    back = []
+    for p, (first, size, axes) in enumerate(PARTS):
+        q, e = size // 4, size // 16
+        a, b, c = axes
+        f2 = first // 16
+        for copy in third[p]:
+            copy.wait_recv()
+        sent += third[p]
+        mine = rows(k * 1024 + first + index[a] * q + index[b] * e, e)
+        total = ((rz[0, f2 : f2 + e] + rz[1, f2 : f2 + e]) + rz[2, f2 : f2 + e]) + rz[3, f2 : f2 + e]
+        new_probe[mine] = probe[mine] - total * scale
+        back.append([push(new_probe.at[mine], new_probe.at[mine], peer) for peer in group[b]])
+    push_over(2)
+    push_side(4)
+    last = []
+    for p, (first, size, axes) in enumerate(PARTS):
+        q = size // 4
+        a, b, c = axes
+        for copy in back[p]:
+            copy.wait_recv()
+        sent += back[p]
+        mine = rows(k * 1024 + first + index[a] * q, q)
+        last.append([push(new_probe.at[mine], new_probe.at[mine], peer) for peer in group[a]])
+    push_over(3)
+    for i in (5, 6, 7):
+        push_side(i)
+    probe_peak = jnp.max(sum(probe[m * n : (m + 1) * n] * probe[m * n : (m + 1) * n] for m in range(8)))
     inverse = 1.0 / probe_peak
-    t3.wait_recv()
-    own[:, 0:n, :] += over[...]
-    new_obj[:, :, n : 2 * n] = tile[:, :, n : 2 * n] - own[:, :, n : 2 * n] * inverse
-    t2.wait_recv()
-    t4.wait_recv()
-    new_obj[:, :, 0:n] = tile[:, :, 0:n] - (own[:, :, 0:n] + side[...]) * inverse
-    for copy in pending + [t1, t2, t3, t4]:
+    new_obj[:, n : 2 * n, n : 2 * n] = obj[:, n : 2 * n, n : 2 * n] - gext[:, n : 2 * n, n : 2 * n] * inverse
+    final = []
+    for p, (first, size, axes) in enumerate(PARTS):
+        for copy in last[p]:
+            copy.wait_recv()
+        sent += last[p]
+        mine = rows(k * 1024 + first, size)
+        final.append(push(new_probe.at[mine], new_probe.at[mine], group["k"][0]))
+    for copy in over_sent:
+        copy.wait_recv()
+    new_obj[:, 0:n, n : 2 * n] = obj[:, 0:n, n : 2 * n] - (gext[:, 0:n, n : 2 * n] + over[:, :, n : 2 * n]) * inverse
+    for copy in side_sent:
+        copy.wait_recv()
+    sent += over_sent + side_sent + corner_sent + swap + final + small.done
+    new_obj[:, 0:n, 0:n] = obj[:, 0:n, 0:n] - (gext[:, 0:n, 0:n] + over[:, :, 0:n] + side[:, 0:n]) * inverse
+    new_obj[:, n : 2 * n, 0:n] = obj[:, n : 2 * n, 0:n] - (gext[:, n : 2 * n, 0:n] + side[:, n : 2 * n]) * inverse
+    for copy in final:
+        copy.wait_recv()
+    for copy in sent:
         copy.wait_send()
 
 
 def exchange(gext, pg, obj, probe, peak, loss):
     V = pl.BlockSpec(memory_space=pltpu.VMEM)
-    A = pl.BlockSpec(memory_space=pl.ANY)
     S = pl.BlockSpec(memory_space=pltpu.SMEM)
-    copies = 14 + 2 * 10
     new_obj, new_probe, loss_mean = pl.pallas_call(
         exchange_kernel,
         out_shape=(
@@ -423,28 +494,23 @@
             jax.ShapeDtypeStruct((2048, 256), F32),
             jax.ShapeDtypeStruct((1, 1), F32),
         ),
-        in_specs=[A, A, A, A, V, V],
+        in_specs=[V] * 6,
         out_specs=(V, V, S),
         scratch_shapes=[
-            pltpu.VMEM((2, 512, 512), F32),
-            pltpu.VMEM((2, 512, 512), F32),
-            pltpu.VMEM((2048, 256), F32),
-            pltpu.VMEM((2048, 256), F32),
             pltpu.VMEM((2, 256, 256), F32),
             pltpu.VMEM((2, 256, 256), F32),
             pltpu.VMEM((2, 256, 512), F32),
             pltpu.VMEM((2, 512, 256), F32),
-            pltpu.VMEM((1, 1024, 256), F32),
+            pltpu.VMEM((1024, 256), F32),
             pltpu.VMEM((3, 256, 256), F32),
             pltpu.VMEM((3, 64, 256), F32),
-            pltpu.VMEM((3, 16, 256), F32),
-            pltpu.VMEM((5, 8, 128), F32),
-            pltpu.VMEM((10, 8, 128), F32),
-            pltpu.SemaphoreType.DMA((5,)),
-            pltpu.SemaphoreType.DMA((copies,)),
-            pltpu.SemaphoreType.DMA((copies,)),
+            pltpu.VMEM((4, 64, 256), F32),
+            pltpu.VMEM((5, 16, 128), F32),
+            pltpu.VMEM((4, 4, 16, 128), F32),
+            pltpu.SemaphoreType.DMA((96,)),
+            pltpu.SemaphoreType.DMA((96,)),
         ],
-        compiler_params=pltpu.CompilerParams(collective_id=1, has_side_effects=True, vmem_limit_bytes=48 << 20),
+        compiler_params=pltpu.CompilerParams(collective_id=1, has_side_effects=True, vmem_limit_bytes=30 << 20),
         name="exchange",
     )(gext, pg.reshape(2048, 256), obj, probe.reshape(2048, 256), peak, loss)
     return new_obj, new_probe.reshape(probe.shape), loss_mean.reshape(())

time: 154 us -> 119 us (0.77)
  Pallas kernels: 143 us -> 103 us
  local copies, waits for them, and re-layouts: 8.35 us -> 13.3 us
    pallas_call x1, Pallas kernels: 24.7 us -> 8.71 us  [compute(): pl.pallas_call(compute_kernel, out_shape=(jax.ShapeDtypeStruct((2, 776, 8...]
    pallas_call x1, Pallas kernels: 44.1 us -> 28.9 us  [halo(): pl.pallas_call(halo_kernel, out_shape=(jax.ShapeDtypeStruct((2, 512, 256)...]
    pallas_call x1, Pallas kernels: 74.4 us -> 65.5 us  [exchange(): pl.pallas_call(exchange_kernel, out_shape=(jax.ShapeDtypeStruct((2, 512,...]
    unnamed x11 -> x25, local copies, waits for them, and re-layouts: 8.35 us -> 13.3 us
where the time goes in v3:
time: 119 us
  Pallas kernels  103 us (87%)
  local copies, waits for them, and re-layouts  13.3 us (11%)
  between operations  2.39 us (2%)
    pallas_call x1, Pallas kernels, exchange(): pl.pallas_call(exchange_kernel, out_shape=(jax.ShapeDtypeStruct((2, 512,...  65.5 us
    pallas_call x1, Pallas kernels, halo(): pl.pallas_call(halo_kernel, out_shape=(jax.ShapeDtypeStruct((2, 512, 256)...  28.9 us
    unnamed x25, local copies, waits for them, and re-layouts  13.3 us
    pallas_call x1, Pallas kernels, compute(): pl.pallas_call(compute_kernel, out_shape=(jax.ShapeDtypeStruct((2, 776, 8...  8.71 us

profile of v3, /device:TPU:1, one launch (start us, length us, event | category | flops | bytes accessed | tf_op | source)
XLA Modules:
  0.0 118.7 jit_solution(11134518139134843062)
XLA Ops:
  0.6 0.0 copy-start.10
  0.6 0.8 copy.13.offsets
  1.4 0.0 copy-start
  1.4 1.6 %copy-done = f32[2,512,512]{2,1,0:T(8,128)S(1)} copy-done((f32[2,512,512]{2,1,0:T(8,128)S(1)}, f32[2,512,512]{2,1,0:T(8,128)}, u32[]{:S(2)}) %copy-start) | copy-done | bytes 2097176
  3.0 0.0 copy-start.1
  3.0 28.9 %halo.1 = (f32[2,512,256]{2,1,0:T(8,128)S(1)}, f32[2,256,768]{2,1,0:T(8,128)S(1)}, f32[8,128]{1,0:T(8,128)S(1)}) custom-call(f32[2,512,512]{2,1,0:T(8,128)S(1)} %copy-done), custom_call_target="tpu_custom_call" | custom-call | tf_op jit(solution)/shard_map/halo/pallas_call | solution.py:301
  31.9 0.0 copy-done.10
  31.9 0.0 copy-done.1
  31.9 0.0 copy-start.2
  31.9 1.6 %copy-done.2 = f32[2,4,256,256]{3,2,1,0:T(8,128)S(1)} copy-done((f32[2,4,256,256]{3,2,1,0:T(8,128)S(1)}, f32[2,4,256,256]{3,2,1,0:T(8,128)}, u32[]{:S(2)}) %copy-start.2) | copy-done | bytes 2097176
  33.5 0.0 copy-start.4
  33.5 1.2 %copy-done.4 = f32[1,4,256,256]{3,2,1,0:T(8,128)S(1)} copy-done((f32[1,4,256,256]{3,2,1,0:T(8,128)S(1)}, f32[1,4,256,256]{3,2,1,0:T(8,128)}, u32[]{:S(2)}) %copy-start.4) | copy-done | bytes 1048600
  34.7 0.0 copy-start.5
  34.7 1.1 copy-done.5
  35.8 0.0 copy-start.6
  35.8 1.1 copy-done.6
  37.0 0.0 copy-start.7
  37.0 1.1 copy-done.7
  38.1 0.0 copy-start.8
  38.1 1.1 copy-done.8
  39.2 0.0 copy-start.9
  39.2 0.9 copy-done.9
  40.1 0.0 copy-start.3
  40.1 8.7 %compute.1 = (f32[2,776,896]{2,1,0:T(8,128)S(1)}, f32[2,4,256,256]{3,2,1,0:T(8,128)S(1)}, f32[8,128]{1,0:T(8,128)S(1)}) custom-call(s32[128]{0:T(128)S(1)} %copy-done.10, s32[1,4,2]{2,1,0:T(4,128)S(1)} %copy.13.offsets, f32[2,512,512]{2,1,0:T(8,128)S(1)} %copy-done.1, f32[2,512,256]{2,1,0:T(8,128)S(1)} %get-tuple-element.12.hr, ...), custom_call_target="tpu_custom_call" | custom-call | tf_op jit(solution)/shard_map/compute/pallas_call | solution.py:169
  48.9 0.0 copy-done.3
  48.9 65.5 %exchange.1 = (f32[2,512,512]{2,1,0:T(8,128)S(1)}, f32[2048,256]{1,0:T(8,128)S(1)}, f32[1,1]{1,0:T(1,128)}) custom-call(f32[2,776,896]{2,1,0:T(8,128)S(1)} %get-tuple-element.14.gext, f32[2048,256]{1,0:T(8,128)S(1)} %bitcast.6, f32[2,512,512]{2,1,0:T(8,128)S(1)} %copy-done.1, f32[2048,256]{1,0:T(8,128)S(1)} %bitcast.4, f32[8,128]{1,0:T(8,128)S(1)} %get-tuple-element.16.peak, ...), custom_call_target="tpu_custom_call" | custom-call | tf_op jit(solution)/shard_map/exchange/pallas_call | solution.py:490
  114.4 1.3 %copy.17 = f32[2,512,512]{2,1,0:T(8,128)} copy(f32[2,512,512]{2,1,0:T(8,128)S(1)} %get-tuple-element.24) | data formatting | bytes 4194304
  115.7 1.3 %copy.18 = f32[2,4,256,256]{3,2,1,0:T(8,128)} copy(f32[2,4,256,256]{3,2,1,0:T(8,128)S(1)} %bitcast.5) | data formatting | bytes 4194304
Async XLA Ops:
  0.6 31.2 %copy-start.10 = (s32[128]{0:T(128)S(1)}, s32[128]{0:T(128)}, u32[]{:S(2)}) copy-start(s32[128]{0:T(128)} %counts.1) | copy-start | bytes 1540
  1.4 1.6 %copy-start = (f32[2,512,512]{2,1,0:T(8,128)S(1)}, f32[2,512,512]{2,1,0:T(8,128)}, u32[]{:S(2)}) copy-start(f32[2,512,512]{2,1,0:T(8,128)} %obj.5) | copy-start | bytes 6291460
  3.0 28.9 %copy-start.1 = (f32[2,512,512]{2,1,0:T(8,128)S(1)}, f32[2,512,512]{2,1,0:T(8,128)}, u32[]{:S(2)}) copy-start(f32[2,512,512]{2,1,0:T(8,128)} %obj.5) | copy-start | bytes 6291460
  31.9 1.6 %copy-start.2 = (f32[2,4,256,256]{3,2,1,0:T(8,128)S(1)}, f32[2,4,256,256]{3,2,1,0:T(8,128)}, u32[]{:S(2)}) copy-start(f32[2,4,256,256]{3,2,1,0:T(8,128)} %probe.1) | copy-start | bytes 6291460
  33.5 1.2 %copy-start.4 = (f32[1,4,256,256]{3,2,1,0:T(8,128)S(1)}, f32[1,4,256,256]{3,2,1,0:T(8,128)}, u32[]{:S(2)}) copy-start(f32[1,4,256,256]{3,2,1,0:T(8,128)} %patterns.1) | copy-start | bytes 3145732
  34.7 1.1 copy-start.5
  35.8 1.1 copy-start.6
  37.0 1.1 copy-start.7
  38.1 1.1 copy-start.8
  39.2 0.9 copy-start.9
  40.1 8.7 %copy-start.3 = (f32[2,4,256,256]{3,2,1,0:T(8,128)S(1)}, f32[2,4,256,256]{3,2,1,0:T(8,128)}, u32[]{:S(2)}) copy-start(f32[2,4,256,256]{3,2,1,0:T(8,128)} %probe.1) | copy-start | bytes 6291460

commit v4 on v3

--- a/solution.py
+++ b/solution.py
@@ -53,98 +53,154 @@
     hi, lo = split(x)
     return dot(jnp.concatenate([hi, lo, hi], axis=1), t)
 
-def compute_kernel(counts, offsets, obj, hr, hb, probe, patterns, left, leftT, right, rightT, perm,
-                   gext, pgrad, loss_ref, ext, patch, psi, res, acc, swap, local):
-    loads = [
-        pltpu.make_async_copy(obj, ext.at[:, 0 : 2 * N, 0 : 2 * N], local.at[0]),
-        pltpu.make_async_copy(hr, ext.at[:, 0 : 2 * N, 2 * N : 3 * N], local.at[1]),
-        pltpu.make_async_copy(hb, ext.at[:, 2 * N : 3 * N, 0 : 3 * N], local.at[2]),
-    ]
-    for load in loads:
-        load.start()
+def twice(a, axis):
+    return jnp.concatenate([a, lax.slice_in_dim(a, 0, N, axis=axis)], axis=axis)
+
+
+def compute_kernel(counts, offsets, ext, probe, pats, left, leftT, right, rightT,
+                   gext, pgrad, loss_ref, patch, psi, res, acc, xa, xb, xc, xd):
     row = lax.axis_index("row")
     col = lax.axis_index("col")
     count = counts[row * 16 + col]
     gext[...] = jnp.zeros_like(gext)
     pgrad[...] = jnp.zeros_like(pgrad)
     loss_ref[...] = jnp.zeros_like(loss_ref)
-    for load in loads:
-        load.wait()
-
-    @pl.when(col == 15)
-    def _():
-        ext[:, :, 2 * N : 3 * N] = jnp.zeros((2, 776, N), jnp.float32)
-
-    @pl.when(row == 7)
-    def _():
-        ext[:, 2 * N : 3 * N, :] = jnp.zeros((2, N, 896), jnp.float32)
 
     def slot(s, _):
-        r = offsets[0, s, 0]
-        c = offsets[0, s, 1]
+        r = offsets[0, 0, s]
+        c = offsets[0, 1, s]
         ca = pl.multiple_of(c // 128 * 128, 128)
         cs = c - ca
         ra = pl.multiple_of(r // 8 * 8, 8)
         rs = r - ra
+        sub = lax.broadcasted_iota(jnp.int32, (1, 8, N), 1)
         for comp in (0, 1):
             x = ext[comp, pl.ds(ra, 264), pl.ds(ca, 384)]
-            x = pltpu.roll(x, 384 - cs, 1)[:, :N]
-            patch[comp] = pltpu.roll(x, 264 - rs, 0)[:N]
-        hi, lo = split(patterns[0, s])
-        y = dot(hi, perm[...]) + dot(lo, perm[...])
-        for q in (0, 1):
-            swap[q] = y[:, q * H:(q + 1) * H]
-        for q in (0, 1):
+            x = pltpu.roll(x, 384 - cs, 1)[:, :N].reshape(33, 8, N)
+            x = pltpu.roll(x, 8 - rs, 1)
+            patch[comp] = jnp.where(sub < 8 - rs, x[:32], x[1:]).reshape(N, N)
+
+        def stage_a(m):
+            for i in range(0, H, 16):
+                er, ei = [], []
+                for t in (i, H + i):
+                    qr, qi = probe[0, m, t : t + 16], probe[1, m, t : t + 16]
+                    xr, xi = patch[0, t : t + 16], patch[1, t : t + 16]
+                    er.append(qr * xr - qi * xi)
+                    ei.append(qr * xi + qi * xr)
+                for p in (0, 1):
+                    for at, e in ((i, er), (H + i, ei)):
+                        hi, lo = split(e[0] + e[1] if p == 0 else e[0] - e[1])
+                        xa[m % 2, p, at : at + 16] = hi
+                        xa[m % 2, p, N + at : N + at + 16] = lo
+
+        def stage_b(m):
+            return [dot(left[p], twice(xa[m % 2, p], 0)) for p in (0, 1)]
+
+        def stage_c(m, L):
             for p in (0, 1):
-                res[q, p * H:(p + 1) * H, :] = -swap[q, pl.ds(p, H, stride=2), :]
-
-        def fwd(m, _):
-            qr, qi, orr, oi = probe[0, m], probe[1, m], patch[0], patch[1]
-            er = qr * orr - qi * oi
-            ei = qr * oi + qi * orr
-            L = []
+                for i in range(0, H, 16):
+                    re, im = L[p][i : i + 16], L[p][H + i : H + i + 16]
+                    at = slice(p * H + i, p * H + i + 16)
+                    for q in (0, 1):
+                        for lane, e in ((0, re), (H, im)):
+                            f = e[:, :H] + e[:, H:] if q == 0 else e[:, :H] - e[:, H:]
+                            hi, lo = split(f)
+                            xb[m % 2, q, at, lane : lane + H] = hi
+                            xb[m % 2, q, at, N + lane : N + lane + H] = lo
+
+        def stage_d(m):
+            return [dot(twice(xb[m % 2, q], 1), rightT[q]) for q in (0, 1)]
+
+        def stage_e(m, X):
+            for q in (0, 1):
+                for i in range(0, N, 16):
+                    x = X[q][i : i + 16]
+                    psi[m, q, i : i + 16] = x
+                    e = x[:, :H] * x[:, :H] + x[:, H:] * x[:, H:]
+                    before = -pats[s, q, i : i + 16] if m == 0 else res[q, i : i + 16]
+                    res[q, i : i + 16] = before + e
+
+        Ls, Xs = {}, {}
+        stage_a(0)
+        for t in range(6):
+            if t < 4:
+                Ls[t] = stage_b(t)
+            if 0 <= t - 1 < 4:
+                Xs[t - 1] = stage_d(t - 1)
+            if t + 1 < 4:
+                stage_a(t + 1)
+            if t < 4:
+                stage_c(t, Ls[t])
+            if 0 <= t - 1 < 4:
+                stage_e(t - 1, Xs[t - 1])
+
+        def stage_f(m):
+            for q in (0, 1):
+                for i in range(0, N, 16):
+                    w = res[q, i : i + 16]
+                    x = psi[m, q, i : i + 16]
+                    for lane in (0, H):
+                        hi, lo = split(x[:, lane : lane + H] * w)
+                        xc[m % 2, q, i : i + 16, lane : lane + H] = hi
+                        xc[m % 2, q, i : i + 16, N + lane : N + lane + H] = lo
+
+        def stage_g(m):
+            return [dot(twice(xc[m % 2, q], 1), right[q]) for q in (0, 1)]
+
+        def stage_i(m, T):
             for p in (0, 1):
-                f = (lambda a: a[:H] + a[H:]) if p == 0 else (lambda a: a[:H] - a[H:])
-                L.append(lmul(left[p], jnp.concatenate([f(er), f(ei)], axis=0)))
-            re = jnp.concatenate([L[0][:H], L[1][:H]], axis=0)
-            im = jnp.concatenate([L[0][H:], L[1][H:]], axis=0)
-            for q in (0, 1):
-                f = (lambda a: a[:, :H] + a[:, H:]) if q == 0 else (lambda a: a[:, :H] - a[:, H:])
-                x = rmul(jnp.concatenate([f(re), f(im)], axis=1), rightT[q])
-                psi[m, q] = x
-                res[q] += x[:, :H] * x[:, :H] + x[:, H:] * x[:, H:]
-            return 0
-        lax.fori_loop(0, 4, fwd, 0, unroll=True)
+                for i in range(0, H, 16):
+                    t0, t1 = T[0][p * H + i : p * H + i + 16], T[1][p * H + i : p * H + i + 16]
+                    for half, x in ((0, t0 + t1), (H, t0 - t1)):
+                        for at, lane in ((i, 0), (H + i, H)):
+                            hi, lo = split(x[:, lane : lane + H])
+                            xd[m % 2, p, at : at + 16, half : half + H] = hi
+                            xd[m % 2, p, N + at : N + at + 16, half : half + H] = lo
+
+        def stage_j(m):
+            return [dot(leftT[p], twice(xd[m % 2, p], 0)) for p in (0, 1)]
+
+        def stage_k(m, L):
+            for i in range(0, H, 8):
+                for h, sign in ((0, 1), (H, -1)):
+                    at = slice(h + i, h + i + 8)
+                    if sign == 1:
+                        br = L[0][i : i + 8] + L[1][i : i + 8]
+                        bi = L[0][H + i : H + i + 8] + L[1][H + i : H + i + 8]
+                    else:
+                        br = L[0][i : i + 8] - L[1][i : i + 8]
+                        bi = L[0][H + i : H + i + 8] - L[1][H + i : H + i + 8]
+                    qr, qi = probe[0, m, at], probe[1, m, at]
+                    xr, xi = patch[0, at], patch[1, at]
+                    gr, gi = qr * br + qi * bi, qr * bi - qi * br
+                    if m:
+                        gr, gi = acc[0, at] + gr, acc[1, at] + gi
+                    acc[0, at] = gr
+                    acc[1, at] = gi
+                    pgrad[0, m, at] += xr * br + xi * bi
+                    pgrad[1, m, at] += xr * bi - xi * br
+
+        Ts, Ls = {}, {}
+        stage_f(0)
         loss_ref[...] += jnp.sum((res[0] * res[0] + res[1] * res[1]).reshape(32, 8, 128), axis=0)
-        acc[...] = jnp.zeros_like(acc)
-
-        def bwd(m, _):
-            t = []
-            for q in (0, 1):
-                R = res[q]
-                t.append(rmul(psi[m, q] * jnp.concatenate([R, R], axis=1), right[q]))
-            x0, x1 = t[0] + t[1], t[0] - t[1]
-            L = []
-            for p in (0, 1):
-                sl = slice(p * H, (p + 1) * H)
-                y = jnp.concatenate([
-                    jnp.concatenate([x0[sl, :H], x1[sl, :H]], axis=1),
-                    jnp.concatenate([x0[sl, H:], x1[sl, H:]], axis=1)], axis=0)
-                L.append(lmul(leftT[p], y))
-            top, bot = L[0] + L[1], L[0] - L[1]
-            for i, b in enumerate((top, bot)):
-                sl = slice(i * H, (i + 1) * H)
-                br, bi = b[:H], b[H:]
-                qr, qi = probe[0, m, sl], probe[1, m, sl]
-                orr, oi = patch[0, sl], patch[1, sl]
-                acc[0, sl, :N] += qr * br + qi * bi
-                acc[1, sl, :N] += qr * bi - qi * br
-                pgrad[0, m, sl] += orr * br + oi * bi
-                pgrad[1, m, sl] += orr * bi - oi * br
-            return 0
-        lax.fori_loop(0, 4, bwd, 0, unroll=True)
+        for t in range(6):
+            if t < 4:
+                Ts[t] = stage_g(t)
+            if 0 <= t - 1 < 4:
+                Ls[t - 1] = stage_j(t - 1)
+            if t + 1 < 4:
+                stage_f(t + 1)
+            if t < 4:
+                stage_i(t, Ts[t])
+            if 0 <= t - 1 < 4:
+                stage_k(t - 1, Ls[t - 1])
+
         for comp in (0, 1):
-            x = pltpu.roll(acc[comp], rs, 0)
+            x = pltpu.roll(acc[comp].reshape(32, 8, N), rs, 1)
+            none = jnp.zeros((1, 8, N), jnp.float32)
+            x = jnp.where(sub < rs, jnp.concatenate([none, x], axis=0), jnp.concatenate([x, none], axis=0))
+            x = jnp.concatenate([x.reshape(264, N), jnp.zeros((264, H), jnp.float32)], axis=1)
             gext[comp, pl.ds(ra, 264), pl.ds(ca, 384)] += pltpu.roll(x, cs, 1)
         return 0
 
@@ -161,32 +217,31 @@
         gext[:, 2 * N : 3 * N, :] = jnp.zeros((2, N, 896), jnp.float32)
 
 
-def compute(counts, offsets, obj, hr, hb, probe, patterns):
-    consts = [jnp.asarray(t) for t in tables()]
+def compute(counts, offsets, ext, probe, pats, *consts):
     V = pl.BlockSpec(memory_space=pltpu.VMEM)
     S = pl.BlockSpec(memory_space=pltpu.SMEM)
-    A = pl.BlockSpec(memory_space=pl.ANY)
     return pl.pallas_call(
         compute_kernel,
         out_shape=(
-            jax.ShapeDtypeStruct((2, 776, 896), jnp.float32),
-            jax.ShapeDtypeStruct((2, 4, N, N), jnp.float32),
+            pltpu.VMEM((2, 776, 896), jnp.float32),
+            pltpu.VMEM((2, 4, N, N), jnp.float32),
             jax.ShapeDtypeStruct((8, 128), jnp.float32),
         ),
-        in_specs=[S, S] + [A] * 3 + [V] * 7,
+        in_specs=[S, S] + [V] * 7,
         out_specs=(V, V, V),
         scratch_shapes=[
-            pltpu.VMEM((2, 776, 896), jnp.float32),
             pltpu.VMEM((2, N, N), jnp.float32),
             pltpu.VMEM((4, 2, N, N), jnp.float32),
             pltpu.VMEM((2, N, H), jnp.float32),
-            pltpu.VMEM((2, 264, 384), jnp.float32),
-            pltpu.VMEM((2, N, H), jnp.float32),
-            pltpu.SemaphoreType.DMA((3,)),
+            pltpu.VMEM((2, N, N), jnp.float32),
+            pltpu.VMEM((2, 2, 2 * N, N), jnp.bfloat16),
+            pltpu.VMEM((2, 2, N, 2 * N), jnp.bfloat16),
+            pltpu.VMEM((2, 2, N, 2 * N), jnp.bfloat16),
+            pltpu.VMEM((2, 2, 2 * N, N), jnp.bfloat16),
         ],
-        compiler_params=pltpu.CompilerParams(vmem_limit_bytes=24 << 20),
+        compiler_params=pltpu.CompilerParams(vmem_limit_bytes=16 << 20),
         name="compute",
-    )(counts, offsets, obj, hr, hb, probe, patterns, *consts)
+    )(counts, offsets, ext, probe, pats, *consts)
 
 
 MESH = pl.DeviceIdType.MESH
@@ -269,65 +324,117 @@
         self.value[self.step] = total
 
 
-def halo_kernel(obj, hr, hb, peak, mine, local, send, recv):
-    own = pltpu.make_async_copy(obj, mine, local.at[0])
-    own.start()
-    left, right, above, below = neighbours()
-    greet(list(neighbours()))
+def halo_kernel(obj, probe, patterns, left_t, left_tt, right_t, right_tt, perm,
+                ext, probe_v, pat_v, left_v, left_tv, right_v, right_tv, peak,
+                raw, sort, swap, relay, local, send, recv):
     n = 256
-    top = remote(obj.at[:, 0:n, 0:n], hr.at[:, 0:n, :], send, recv, 0, left)
-    side = remote(obj.at[:, 0:n, :], hb.at[:, :, 0 : 2 * n], send, recv, 2, above)
-    bottom = remote(obj.at[:, n : 2 * n, 0:n], hr.at[:, n : 2 * n, :], send, recv, 1, left)
-    own.wait()
+    west, east, above, below = neighbours()
+    x, y, z, k = place()
+    up = device_at(x, y, z + 1, k)
+    down = device_at(x, y, z - 1, k)
+    end = device_at(x - jnp.where(z == 2, 1, 0), y, z + 1, k)
+    origin = device_at(x + jnp.where(z == 3, 1, 0), y, z - 1, k)
+    pairs = [
+        (probe, probe_v), (patterns.at[0], raw), (perm, sort), (left_t, left_v), (left_tt, left_tv),
+        (right_t, right_v), (right_tt, right_tv), (obj, ext.at[:, 0 : 2 * n, 0 : 2 * n]),
+    ]
+    loads = [pltpu.make_async_copy(src, dst, local.at[i]) for i, (src, dst) in enumerate(pairs)]
+    greet([west, east, above, below, up, down, end, origin])
+    top = remote(obj.at[:, 0:n, 0:n], ext.at[:, 0:n, 2 * n : 3 * n], send, recv, 0, west)
+    side = remote(obj.at[:, 0:n, :], ext.at[:, 2 * n : 3 * n, 0 : 2 * n], send, recv, 2, above)
+    first = [
+        remote(obj.at[:, 384 + 64 * i : 448 + 64 * i, 0:n], relay.at[0, i], send, recv, 4 + i, up) for i in (0, 1)
+    ]
+    middle = remote(obj.at[:, n:384, 0:n], ext.at[:, n:384, 2 * n : 3 * n], send, recv, 1, west)
+    for load in loads:
+        load.start()
+    for load in loads:
+        load.wait()
 
     def largest(i, best):
-        re = mine[0, pl.ds(pl.multiple_of(i * 16, 16), 16), :]
-        im = mine[1, pl.ds(pl.multiple_of(i * 16, 16), 16), :]
+        at = pl.ds(pl.multiple_of(i * 16, 16), 16)
+        re = ext[0, at, 0 : 2 * n]
+        im = ext[1, at, 0 : 2 * n]
         return jnp.maximum(best, re * re + im * im)
 
     best = lax.fori_loop(0, 32, largest, jnp.zeros((16, 512), F32))
     peak[...] = jnp.full((8, 128), jnp.max(best), F32)
+
+    def order(s, _):
+        hi, lo = split(raw[s])
+        both = dot(hi, sort[...]) + dot(lo, sort[...])
+        for q in (0, 1):
+            swap[q] = both[:, q * H : (q + 1) * H]
+        for q in (0, 1):
+            for p in (0, 1):
+                pat_v[s, q, p * H : (p + 1) * H, :] = swap[q, pl.ds(p, H, stride=2), :]
+        return 0
+
+    lax.fori_loop(0, 4, order, 0)
+    second = []
+    for i in (0, 1):
+        first[i].wait_recv()
+        second.append(remote(relay.at[0, i], relay.at[1, i], send, recv, 6 + i, up))
     top.wait_recv()
-    corner = remote(hr.at[:, 0:n, :], hb.at[:, :, 2 * n : 3 * n], send, recv, 3, above)
-    top.wait_send()
-    side.wait()
-    corner.wait()
-    bottom.wait()
-
-
-def halo(obj):
+    corner = remote(ext.at[:, 0:n, 2 * n : 3 * n], ext.at[:, 2 * n : 3 * n, 2 * n : 3 * n], send, recv, 3, above)
+    third = []
+    for i in (0, 1):
+        second[i].wait_recv()
+        m = pl.ds(384 + 64 * i, 64)
+        third.append(remote(relay.at[1, i], ext.at[:, m, 2 * n : 3 * n], send, recv, 8 + i, end))
+    for copy in (side, middle, corner, *third):
+        copy.wait_recv()
+    for copy in (top, side, middle, corner, *first, *second, *third):
+        copy.wait_send()
+
+    @pl.when(lax.axis_index("col") == 15)
+    def _():
+        ext[:, :, 2 * n : 3 * n] = jnp.zeros((2, 776, n), F32)
+
+    @pl.when(lax.axis_index("row") == 7)
+    def _():
+        ext[:, 2 * n : 3 * n, :] = jnp.zeros((2, n, 896), F32)
+
+
+def halo(obj, probe, patterns):
     V = pl.BlockSpec(memory_space=pltpu.VMEM)
-    A = pl.BlockSpec(memory_space=pl.ANY)
+    A = pl.BlockSpec(memory_space=pltpu.HBM)
+    consts = [jnp.asarray(t) for t in tables()]
+    ins = [pltpu.with_memory_space_constraint(t, pltpu.HBM) for t in (obj, probe, patterns, *consts)]
+    shapes = [(2, 776, 896), (2, 4, N, N), (4, 2, N, H)]
+    outs = [pltpu.VMEM(s, F32) for s in shapes] + [pltpu.VMEM(t.shape, t.dtype) for t in consts[:4]]
     return pl.pallas_call(
         halo_kernel,
-        out_shape=(
-            jax.ShapeDtypeStruct((2, 512, 256), F32),
-            jax.ShapeDtypeStruct((2, 256, 768), F32),
-            jax.ShapeDtypeStruct((8, 128), F32),
-        ),
-        in_specs=[pl.BlockSpec(memory_space=pltpu.HBM)],
-        out_specs=(A, A, V),
+        out_shape=tuple(outs) + (jax.ShapeDtypeStruct((8, 128), F32),),
+        in_specs=[A] * 8,
+        out_specs=(V,) * 8,
         scratch_shapes=[
-            pltpu.VMEM((2, 512, 512), F32),
-            pltpu.SemaphoreType.DMA((1,)),
-            pltpu.SemaphoreType.DMA((4,)),
-            pltpu.SemaphoreType.DMA((4,)),
+            pltpu.VMEM((4, N, N), F32),
+            pltpu.VMEM((N, N), jnp.bfloat16),
+            pltpu.VMEM((2, N, H), F32),
+            pltpu.VMEM((2, 2, 2, 64, N), F32),
+            pltpu.SemaphoreType.DMA((8,)),
+            pltpu.SemaphoreType.DMA((10,)),
+            pltpu.SemaphoreType.DMA((10,)),
         ],
-        compiler_params=pltpu.CompilerParams(collective_id=0, has_side_effects=True, vmem_limit_bytes=6 << 20),
+        compiler_params=pltpu.CompilerParams(collective_id=0, has_side_effects=True, vmem_limit_bytes=16 << 20),
         name="halo",
-    )(obj)
-
-
-PARTS = ((0, 384, "xyz"), (384, 384, "yzx"), (768, 256, "zxy"))
+    )(*ins)
+
+
+PARTS = ((0, 384, "xyz"), (384, 256, "yzx"), (640, 384, "zxy"))
 
 
 def exchange_kernel(gext, pg, obj, probe, peak, loss, new_obj, new_probe, loss_mean,
-                    strip, corner, over, side, r0, r1, r2, rz, value, slots, send, recv):
+                    strip, corner, over, side, relay, r0, r1, r2, rz, value, slots, send, recv):
     n = 256
     left, right, above, below = neighbours()
     group = groups()
     x, y, z, k = place()
     index = {"x": x, "y": y, "z": z, "k": k}
+    up, down = device_at(x, y, z + 1, k), device_at(x, y, z - 1, k)
+    end = device_at(x + jnp.where(z == 1, 1, 0), y, z - 1, k)
+    origin = device_at(x - jnp.where(z == 0, 1, 0), y, z + 1, k)
     counter = [0]
 
     def push(src, dst, peer):
@@ -341,10 +448,10 @@
         first = lax.broadcasted_iota(jnp.int32, (16, 128), 0) < 8
         return jnp.where(first, a + b, jnp.maximum(a, b))
 
-    everyone = [group[a][i] for a in "kxyz" for i in range(len(group[a]))] + [left, right, above, below]
+    everyone = [group[a][i] for a in "kxyz" for i in range(len(group[a]))] + [left, right, above, below, up, down, end, origin]
     greet(everyone)
     sent = []
-    over_sent, side_sent, corner_sent = [], [], []
+    over_sent, side_sent, corner_sent, rounds = [], [], [], ([], [], [])
 
     def push_corner(i):
         m = pl.ds(2 * n + 128 * i, 128)
@@ -355,12 +462,17 @@
         over_sent.append(push(gext.at[:, m, 0 : 2 * n], over.at[:, 64 * i : 64 * i + 64], below))
 
     def push_side(i):
-        if i < 4:
-            m = pl.ds(n + 64 * i, 64)
-            side_sent.append(push(gext.at[:, m, 2 * n : 3 * n], side.at[:, m], right))
-        else:
-            m = pl.ds(64 * i - n, 64)
-            side_sent.append(push(strip.at[:, m], side.at[:, m], right))
+        m = pl.ds(n + 64 * i, 64) if i < 2 else pl.ds(64 * i - 128, 64)
+        source = gext.at[:, m, 2 * n : 3 * n] if i < 2 else strip.at[:, m]
+        side_sent.append(push(source, side.at[:, m], right))
+
+    def push_round(step, i):
+        m = pl.ds(384 + 64 * i, 64)
+        source = gext.at[:, m, 2 * n : 3 * n] if step == 0 else relay.at[step - 1, i]
+        target = side.at[:, m] if step == 2 else relay.at[step, i]
+        if step:
+            rounds[step - 1][i].wait_recv()
+        rounds[step].append(push(source, target, end if step == 2 else down))
 
     def fold_corner(i):
         corner_sent[i].wait_recv()
@@ -372,6 +484,7 @@
         swap.append(push(pg.at[rows((1 - k) * 1024 + first, size)], r0.at[first : first + size], group["k"][0]))
     push_corner(0)
     push_side(0)
+    push_round(0, 0)
     value[0, 0:8] = loss[...]
     value[0, 8:16] = peak[...]
     small = Small(op, value, slots, send, recv, 84)
@@ -392,6 +505,7 @@
     small.start()
     push_corner(1)
     push_side(1)
+    push_round(0, 1)
     second = []
     for p, (first, size, axes) in enumerate(PARTS):
         q, e = size // 4, size // 16
@@ -410,7 +524,10 @@
     small.finish()
     small.start()
     push_over(0)
+    fold_corner(0)
     push_side(2)
+    push_round(1, 0)
+    push_round(1, 1)
     third = []
     for p, (first, size, axes) in enumerate(PARTS):
         q, e = size // 4, size // 16
@@ -427,9 +544,8 @@
     small.finish()
     small.start()
     push_over(1)
+    fold_corner(1)
     push_side(3)
-    fold_corner(0)
-    fold_corner(1)
     small.finish()
     loss_mean[0, 0] = jnp.sum(value[4, 0:8])
     scale = 1.0 / value[4, 8:9, 0:1]
@@ -448,6 +564,8 @@
         back.append([push(new_probe.at[mine], new_probe.at[mine], peer) for peer in group[b]])
     push_over(2)
     push_side(4)
+    push_round(2, 0)
+    push_round(2, 1)
     last = []
     for p, (first, size, axes) in enumerate(PARTS):
         q = size // 4
@@ -458,8 +576,7 @@
         mine = rows(k * 1024 + first + index[a] * q, q)
         last.append([push(new_probe.at[mine], new_probe.at[mine], peer) for peer in group[a]])
     push_over(3)
-    for i in (5, 6, 7):
-        push_side(i)
+    push_side(5)
     probe_peak = jnp.max(sum(probe[m * n : (m + 1) * n] * probe[m * n : (m + 1) * n] for m in range(8)))
     inverse = 1.0 / probe_peak
     new_obj[:, n : 2 * n, n : 2 * n] = obj[:, n : 2 * n, n : 2 * n] - gext[:, n : 2 * n, n : 2 * n] * inverse
@@ -473,9 +590,9 @@
     for copy in over_sent:
         copy.wait_recv()
     new_obj[:, 0:n, n : 2 * n] = obj[:, 0:n, n : 2 * n] - (gext[:, 0:n, n : 2 * n] + over[:, :, n : 2 * n]) * inverse
-    for copy in side_sent:
+    for copy in side_sent + rounds[2]:
         copy.wait_recv()
-    sent += over_sent + side_sent + corner_sent + swap + final + small.done
+    sent += over_sent + side_sent + rounds[0] + rounds[1] + rounds[2] + corner_sent + swap + final + small.done
     new_obj[:, 0:n, 0:n] = obj[:, 0:n, 0:n] - (gext[:, 0:n, 0:n] + over[:, :, 0:n] + side[:, 0:n]) * inverse
     new_obj[:, n : 2 * n, 0:n] = obj[:, n : 2 * n, 0:n] - (gext[:, n : 2 * n, 0:n] + side[:, n : 2 * n]) * inverse
     for copy in final:
@@ -501,6 +618,7 @@
             pltpu.VMEM((2, 256, 256), F32),
             pltpu.VMEM((2, 256, 512), F32),
             pltpu.VMEM((2, 512, 256), F32),
+            pltpu.VMEM((2, 2, 2, 64, 256), F32),
             pltpu.VMEM((1024, 256), F32),
             pltpu.VMEM((3, 256, 256), F32),
             pltpu.VMEM((3, 64, 256), F32),
@@ -517,9 +635,9 @@
 
 
 def body(object_slab, probe_field, patterns, offsets, counts):
-    hr, hb, peak = halo(object_slab)
-    gext, pg, loss = compute(counts, offsets, object_slab, hr, hb, probe_field, patterns)
-    return exchange(gext, pg, object_slab, probe_field, peak, loss)
+    ext, probe, pats, left, left_t, right, right_t, peak = halo(object_slab, probe_field, patterns)
+    gext, pg, loss = compute(counts, jnp.swapaxes(offsets, 1, 2), ext, probe, pats, left, left_t, right, right_t)
+    return exchange(gext, pg, ext, probe, peak, loss)
 
 
 def solution(mesh):

time: 119 us -> 98.7 us (0.83)
  local copies, waits for them, and re-layouts: 13.3 us -> 2.65 us
  Pallas kernels: 103 us -> 93.5 us
    pallas_call x1, Pallas kernels: 65.5 us -> 52.6 us  [exchange(): pl.pallas_call(exchange_kernel, out_shape=(jax.ShapeDtypeStruct((2, 512,...]
    unnamed x25 -> x6, local copies, waits for them, and re-layouts: 13.3 us -> 2.65 us
    pallas_call x2, Pallas kernels: 37.6 us -> 40.9 us  [the longest x1 27.7 us: halo(): pl.pallas_call(halo_kernel, out_shape=tuple(outs) + (jax.ShapeDtypeStruct...]
where the time goes in v4:
time: 98.7 us; the launch traced here: 98.5 us
  Pallas kernels  93.5 us (95%)
  local copies, waits for them, and re-layouts  2.65 us (3%)
  between operations  2.44 us (2%)
    pallas_call x1, Pallas kernels, exchange(): pl.pallas_call(exchange_kernel, out_shape=(jax.ShapeDtypeStruct((2, 512,...  52.6 us
    pallas_call x1, Pallas kernels, halo(): pl.pallas_call(halo_kernel, out_shape=tuple(outs) + (jax.ShapeDtypeStruct...  27.7 us
    pallas_call x1, Pallas kernels, compute(): pl.pallas_call(compute_kernel, out_shape=(pltpu.VMEM((2, 776, 896), jnp.f...  13.2 us
    unnamed x6, local copies, waits for them, and re-layouts  2.65 us

profile of v4, /device:TPU:1, one launch (start us, length us, event | category | flops | bytes accessed | tf_op | source)
XLA Modules:
  0.0 98.5 jit_solution(15094561369323856237)
XLA Ops:
  0.6 0.0 copy-start
  0.6 0.0 copy-start.1
  0.7 27.7 %halo.1 = (f32[2,776,896]{2,1,0:T(8,128)S(1)}, f32[2,4,256,256]{3,2,1,0:T(8,128)S(1)}, f32[4,2,256,128]{3,2,1,0:T(8,128)S(1)}, bf16[2,256,768]{2,1,0:T(8,128)(2,...) custom-call(f32[2,512,512]{2,1,0:T(8,128)} %obj.1, ...), custom_call_target="tpu_custom_call" | custom-call | tf_op jit(solution)/shard_map/halo/pallas_call | solution.py:406
  28.3 0.0 copy-done
  28.3 0.0 copy-done.1
  28.3 13.2 %compute.1 = (f32[2,776,896]{2,1,0:T(8,128)S(1)}, f32[2,4,256,256]{3,2,1,0:T(8,128)S(1)}, f32[8,128]{1,0:T(8,128)S(1)}) custom-call(s32[128]{0:T(128)S(1)} %copy-done.1, s32[1,2,4]{2,1,0:T(2,128)S(1)} %bitcast.8, f32[2,776,896]{2,1,0:T(8,128)S(1)} %get-tuple-element.17.ext.obj, f32[2,4,256,256]{3,2,1,0:T(8,128)S(1)} %get-tuple-element.18.probe, ...), custom_call_target="tpu_custom_call" | custom-call | tf_op jit(solution)/shard_map/compute/pallas_call | solution.py:223
  41.6 52.6 %exchange.1 = (f32[2,512,512]{2,1,0:T(8,128)S(1)}, f32[2048,256]{1,0:T(8,128)S(1)}, f32[1,1]{1,0:T(1,128)}) custom-call(f32[2,776,896]{2,1,0:T(8,128)S(1)} %get-tuple-element.24.gext, f32[2048,256]{1,0:T(8,128)S(1)} %bitcast.7, f32[2,776,896]{2,1,0:T(8,128)S(1)} %get-tuple-element.17.ext.obj, f32[2048,256]{1,0:T(8,128)S(1)} %bitcast.5, ...), custom_call_target="tpu_custom_call" | custom-call | tf_op jit(solution)/shard_map/exchange/pallas_call | solution.py:607
  94.2 1.3 %copy.16 = f32[2,512,512]{2,1,0:T(8,128)} copy(f32[2,512,512]{2,1,0:T(8,128)S(1)} %get-tuple-element.34) | data formatting | bytes 4194304
  95.5 1.3 %copy.17 = f32[2,4,256,256]{3,2,1,0:T(8,128)} copy(f32[2,4,256,256]{3,2,1,0:T(8,128)S(1)} %bitcast.6) | data formatting | bytes 4194304
Async XLA Ops:
  0.6 27.7 %copy-start = (s32[1,4,2]{1,2,0:T(2,128)S(1)}, s32[1,4,2]{1,2,0:T(2,128)}, u32[]{:S(2)}) copy-start(s32[1,4,2]{1,2,0:T(2,128)} %param.13) | copy-start | bytes 100
  0.6 27.7 %copy-start.1 = (s32[128]{0:T(128)S(1)}, s32[128]{0:T(128)}, u32[]{:S(2)}) copy-start(s32[128]{0:T(128)} %counts.1) | copy-start | bytes 1540

commit v5 on v4

--- a/solution.py
+++ b/solution.py
@@ -57,13 +57,11 @@
     return jnp.concatenate([a, lax.slice_in_dim(a, 0, N, axis=axis)], axis=axis)
 
 
-def compute_kernel(counts, offsets, ext, probe, pats, left, leftT, right, rightT,
+def compute_kernel(counts, offsets, ext, probe, pats, left, leftT, right, rightT, gext_in, pgrad_in,
                    gext, pgrad, loss_ref, patch, psi, res, acc, xa, xb, xc, xd):
     row = lax.axis_index("row")
     col = lax.axis_index("col")
     count = counts[row * 16 + col]
-    gext[...] = jnp.zeros_like(gext)
-    pgrad[...] = jnp.zeros_like(pgrad)
     loss_ref[...] = jnp.zeros_like(loss_ref)
 
     def slot(s, _):
@@ -73,12 +71,15 @@
         cs = c - ca
         ra = pl.multiple_of(r // 8 * 8, 8)
         rs = r - ra
-        sub = lax.broadcasted_iota(jnp.int32, (1, 8, N), 1)
+        sub = lax.broadcasted_iota(jnp.int32, (1, 8, H), 1)
+        lane = lax.broadcasted_iota(jnp.int32, (1, H), 1)
         for comp in (0, 1):
             x = ext[comp, pl.ds(ra, 264), pl.ds(ca, 384)]
-            x = pltpu.roll(x, 384 - cs, 1)[:, :N].reshape(33, 8, N)
-            x = pltpu.roll(x, 8 - rs, 1)
-            patch[comp] = jnp.where(sub < 8 - rs, x[:32], x[1:]).reshape(N, N)
+            x = [pltpu.roll(x[:, i * H : i * H + H], H - cs, 1) for i in range(3)]
+            for i in range(2):
+                y = jnp.where(lane < H - cs, x[i], x[i + 1]).reshape(33, 8, H)
+                y = pltpu.roll(y, 8 - rs, 1)
+                patch[comp, :, i * H : i * H + H] = jnp.where(sub < 8 - rs, y[:32], y[1:]).reshape(N, H)
 
         def stage_a(m):
             for i in range(0, H, 16):
@@ -197,11 +198,17 @@
                 stage_k(t - 1, Ls[t - 1])
 
         for comp in (0, 1):
-            x = pltpu.roll(acc[comp].reshape(32, 8, N), rs, 1)
-            none = jnp.zeros((1, 8, N), jnp.float32)
-            x = jnp.where(sub < rs, jnp.concatenate([none, x], axis=0), jnp.concatenate([x, none], axis=0))
-            x = jnp.concatenate([x.reshape(264, N), jnp.zeros((264, H), jnp.float32)], axis=1)
-            gext[comp, pl.ds(ra, 264), pl.ds(ca, 384)] += pltpu.roll(x, cs, 1)
+            none = jnp.zeros((1, 8, H), jnp.float32)
+            blank = jnp.zeros((264, H), jnp.float32)
+            x = []
+            for i in range(2):
+                y = pltpu.roll(acc[comp, :, i * H : i * H + H].reshape(32, 8, H), rs, 1)
+                y = jnp.where(sub < rs, jnp.concatenate([none, y], axis=0), jnp.concatenate([y, none], axis=0))
+                x.append(pltpu.roll(y.reshape(264, H), cs, 1))
+            x = [blank, x[0], x[1], blank]
+            for i in range(3):
+                at = pl.ds(pl.multiple_of(ca + i * H, H), H)
+                gext[comp, pl.ds(ra, 264), at] += jnp.where(lane < cs, x[i], x[i + 1])
         return 0
 
     lax.fori_loop(0, count, slot, 0)
@@ -227,8 +234,9 @@
             pltpu.VMEM((2, 4, N, N), jnp.float32),
             jax.ShapeDtypeStruct((8, 128), jnp.float32),
         ),
-        in_specs=[S, S] + [V] * 7,
+        in_specs=[S, S] + [V] * 9,
         out_specs=(V, V, V),
+        input_output_aliases={9: 0, 10: 1},
         scratch_shapes=[
             pltpu.VMEM((2, N, N), jnp.float32),
             pltpu.VMEM((4, 2, N, N), jnp.float32),
@@ -325,7 +333,7 @@
 
 
 def halo_kernel(obj, probe, patterns, left_t, left_tt, right_t, right_tt, perm,
-                ext, probe_v, pat_v, left_v, left_tv, right_v, right_tv, peak,
+                ext, probe_v, pat_v, left_v, left_tv, right_v, right_tv, gext, pgrad, peak,
                 raw, sort, swap, relay, local, send, recv):
     n = 256
     west, east, above, below = neighbours()
@@ -340,7 +348,10 @@
     ]
     loads = [pltpu.make_async_copy(src, dst, local.at[i]) for i, (src, dst) in enumerate(pairs)]
     greet([west, east, above, below, up, down, end, origin])
-    top = remote(obj.at[:, 0:n, 0:n], ext.at[:, 0:n, 2 * n : 3 * n], send, recv, 0, west)
+    top = [
+        remote(obj.at[:, m : m + H, 0:n], ext.at[:, m : m + H, 2 * n : 3 * n], send, recv, i, west)
+        for i, m in ((0, 0), (3, H))
+    ]
     side = remote(obj.at[:, 0:n, :], ext.at[:, 2 * n : 3 * n, 0 : 2 * n], send, recv, 2, above)
     first = [
         remote(obj.at[:, 384 + 64 * i : 448 + 64 * i, 0:n], relay.at[0, i], send, recv, 4 + i, up) for i in (0, 1)
@@ -348,6 +359,8 @@
     middle = remote(obj.at[:, n:384, 0:n], ext.at[:, n:384, 2 * n : 3 * n], send, recv, 1, west)
     for load in loads:
         load.start()
+    gext[...] = jnp.zeros_like(gext)
+    pgrad[...] = jnp.zeros_like(pgrad)
     for load in loads:
         load.wait()
 
@@ -371,20 +384,26 @@
         return 0
 
     lax.fori_loop(0, 4, order, 0)
-    second = []
+    second, corner = [], []
     for i in (0, 1):
         first[i].wait_recv()
         second.append(remote(relay.at[0, i], relay.at[1, i], send, recv, 6 + i, up))
-    top.wait_recv()
-    corner = remote(ext.at[:, 0:n, 2 * n : 3 * n], ext.at[:, 2 * n : 3 * n, 2 * n : 3 * n], send, recv, 3, above)
+        top[i].wait_recv()
+        m = i * H
+        corner.append(
+            remote(
+                ext.at[:, m : m + H, 2 * n : 3 * n], ext.at[:, 2 * n + m : 2 * n + m + H, 2 * n : 3 * n],
+                send, recv, 10 + i, above,
+            )
+        )
     third = []
     for i in (0, 1):
         second[i].wait_recv()
         m = pl.ds(384 + 64 * i, 64)
         third.append(remote(relay.at[1, i], ext.at[:, m, 2 * n : 3 * n], send, recv, 8 + i, end))
-    for copy in (side, middle, corner, *third):
+    for copy in (side, middle, *corner, *third):
         copy.wait_recv()
-    for copy in (top, side, middle, corner, *first, *second, *third):
+    for copy in (*top, side, middle, *corner, *first, *second, *third):
         copy.wait_send()
 
     @pl.when(lax.axis_index("col") == 15)
@@ -403,26 +422,27 @@
     ins = [pltpu.with_memory_space_constraint(t, pltpu.HBM) for t in (obj, probe, patterns, *consts)]
     shapes = [(2, 776, 896), (2, 4, N, N), (4, 2, N, H)]
     outs = [pltpu.VMEM(s, F32) for s in shapes] + [pltpu.VMEM(t.shape, t.dtype) for t in consts[:4]]
+    outs += [pltpu.VMEM(s, F32) for s in shapes[:2]]
     return pl.pallas_call(
         halo_kernel,
         out_shape=tuple(outs) + (jax.ShapeDtypeStruct((8, 128), F32),),
         in_specs=[A] * 8,
-        out_specs=(V,) * 8,
+        out_specs=(V,) * 10,
         scratch_shapes=[
             pltpu.VMEM((4, N, N), F32),
             pltpu.VMEM((N, N), jnp.bfloat16),
             pltpu.VMEM((2, N, H), F32),
             pltpu.VMEM((2, 2, 2, 64, N), F32),
             pltpu.SemaphoreType.DMA((8,)),
-            pltpu.SemaphoreType.DMA((10,)),
-            pltpu.SemaphoreType.DMA((10,)),
+            pltpu.SemaphoreType.DMA((12,)),
+            pltpu.SemaphoreType.DMA((12,)),
         ],
         compiler_params=pltpu.CompilerParams(collective_id=0, has_side_effects=True, vmem_limit_bytes=16 << 20),
         name="halo",
     )(*ins)
 
 
-PARTS = ((0, 384, "xyz"), (384, 256, "yzx"), (640, 384, "zxy"))
+PARTS = ((0, 128, "xyz"), (128, 128, "yzx"), (256, 128, "zxy"), (384, 256, "xyz"), (640, 128, "yzx"), (768, 256, "zxy"))
 
 
 def exchange_kernel(gext, pg, obj, probe, peak, loss, new_obj, new_probe, loss_mean,
@@ -487,7 +507,7 @@
     push_round(0, 0)
     value[0, 0:8] = loss[...]
     value[0, 8:16] = peak[...]
-    small = Small(op, value, slots, send, recv, 84)
+    small = Small(op, value, slots, send, recv, 200)
     small.start()
 
     steps = []
@@ -568,13 +588,16 @@
     push_round(2, 1)
     last = []
     for p, (first, size, axes) in enumerate(PARTS):
-        q = size // 4
+        q, e = size // 4, size // 16
         a, b, c = axes
-        for copy in back[p]:
-            copy.wait_recv()
+        copies = []
+        for d in range(4):
+            if d:
+                back[p][d - 1].wait_recv()
+            mine = rows(k * 1024 + first + index[a] * q + lax.rem(index[b] + 4 - d, 4) * e, e)
+            copies.append([push(new_probe.at[mine], new_probe.at[mine], peer) for peer in group[a]])
         sent += back[p]
-        mine = rows(k * 1024 + first + index[a] * q, q)
-        last.append([push(new_probe.at[mine], new_probe.at[mine], peer) for peer in group[a]])
+        last.append(copies)
     push_over(3)
     push_side(5)
     probe_peak = jnp.max(sum(probe[m * n : (m + 1) * n] * probe[m * n : (m + 1) * n] for m in range(8)))
@@ -582,11 +605,16 @@
     new_obj[:, n : 2 * n, n : 2 * n] = obj[:, n : 2 * n, n : 2 * n] - gext[:, n : 2 * n, n : 2 * n] * inverse
     final = []
     for p, (first, size, axes) in enumerate(PARTS):
-        for copy in last[p]:
-            copy.wait_recv()
-        sent += last[p]
-        mine = rows(k * 1024 + first, size)
-        final.append(push(new_probe.at[mine], new_probe.at[mine], group["k"][0]))
+        q = size // 4
+        a, b, c = axes
+        for d in range(4):
+            if d:
+                for copies in last[p]:
+                    copies[d - 1].wait_recv()
+            mine = rows(k * 1024 + first + lax.rem(index[a] + 4 - d, 4) * q, q)
+            final.append(push(new_probe.at[mine], new_probe.at[mine], group["k"][0]))
+        for copies in last[p]:
+            sent += copies
     for copy in over_sent:
         copy.wait_recv()
     new_obj[:, 0:n, n : 2 * n] = obj[:, 0:n, n : 2 * n] - (gext[:, 0:n, n : 2 * n] + over[:, :, n : 2 * n]) * inverse
@@ -607,8 +635,8 @@
     new_obj, new_probe, loss_mean = pl.pallas_call(
         exchange_kernel,
         out_shape=(
-            jax.ShapeDtypeStruct((2, 512, 512), F32),
-            jax.ShapeDtypeStruct((2048, 256), F32),
+            pltpu.VMEM((2, 512, 512), F32),
+            pltpu.VMEM((2048, 256), F32),
             jax.ShapeDtypeStruct((1, 1), F32),
         ),
         in_specs=[V] * 6,
@@ -625,19 +653,55 @@
             pltpu.VMEM((4, 64, 256), F32),
             pltpu.VMEM((5, 16, 128), F32),
             pltpu.VMEM((4, 4, 16, 128), F32),
-            pltpu.SemaphoreType.DMA((96,)),
-            pltpu.SemaphoreType.DMA((96,)),
+            pltpu.SemaphoreType.DMA((212,)),
+            pltpu.SemaphoreType.DMA((212,)),
         ],
         compiler_params=pltpu.CompilerParams(collective_id=1, has_side_effects=True, vmem_limit_bytes=30 << 20),
         name="exchange",
     )(gext, pg.reshape(2048, 256), obj, probe.reshape(2048, 256), peak, loss)
-    return new_obj, new_probe.reshape(probe.shape), loss_mean.reshape(())
+    return new_obj, new_probe, loss_mean
+
+
+def finish_kernel(new_obj, new_probe, loss_mean, obj_out, probe_out, loss_out, sems):
+    copies = []
+    for i in range(4):
+        m = pl.ds(128 * i, 128)
+        copies.append(pltpu.make_async_copy(new_obj.at[:, m], obj_out.at[:, m], sems.at[i]))
+        m = pl.ds(512 * i, 512)
+        copies.append(pltpu.make_async_copy(new_probe.at[m], probe_out.at[m], sems.at[4 + i]))
+    for copy in copies:
+        copy.start()
+    loss_out[0, 0] = loss_mean[0, 0]
+    for copy in copies:
+        copy.wait()
+
+
+def finish(new_obj, new_probe, loss_mean):
+    V = pl.BlockSpec(memory_space=pltpu.VMEM)
+    A = pl.BlockSpec(memory_space=pltpu.HBM)
+    S = pl.BlockSpec(memory_space=pltpu.SMEM)
+    return pl.pallas_call(
+        finish_kernel,
+        out_shape=(
+            pltpu.HBM(new_obj.shape, F32),
+            pltpu.HBM(new_probe.shape, F32),
+            jax.ShapeDtypeStruct((1, 1), F32),
+        ),
+        in_specs=[V, V, S],
+        out_specs=(A, A, S),
+        scratch_shapes=[pltpu.SemaphoreType.DMA((8,))],
+        compiler_params=pltpu.CompilerParams(vmem_limit_bytes=6 << 20),
+        name="finish",
+    )(new_obj, new_probe, loss_mean)
 
 
 def body(object_slab, probe_field, patterns, offsets, counts):
-    ext, probe, pats, left, left_t, right, right_t, peak = halo(object_slab, probe_field, patterns)
-    gext, pg, loss = compute(counts, jnp.swapaxes(offsets, 1, 2), ext, probe, pats, left, left_t, right, right_t)
-    return exchange(gext, pg, ext, probe, peak, loss)
+    ext, probe, pats, left, left_t, right, right_t, gext, pg, peak = halo(object_slab, probe_field, patterns)
+    gext, pg, loss = compute(
+        counts, jnp.swapaxes(offsets, 1, 2), ext, probe, pats, left, left_t, right, right_t, gext, pg
+    )
+    new_obj, new_probe, loss_mean = finish(*exchange(gext, pg, ext, probe, peak, loss))
+    return new_obj, new_probe.reshape(probe_field.shape), loss_mean.reshape(())
 
 
 def solution(mesh):

time: 98.7 us -> 96.3 us (0.976)
  Pallas kernels: 93.5 us -> 96.2 us
  local copies, waits for them, and re-layouts: 2.65 us -> 0.01 us
  between operations: 2.44 us -> 0.69 us
    pallas_call x1 -> x2, Pallas kernels: 52.6 us -> 56.2 us  [the longest x1 53 us: exchange(): pl.pallas_call(exchange_kernel, out_shape=(pltpu.VMEM((2, 512, 512), F32)...]
    unnamed x6 -> x4, local copies, waits for them, and re-layouts: 2.65 us -> 0.01 us
where the time goes in v5:
time: 96.3 us; the launch traced here: 96.9 us
  Pallas kernels  96.2 us (100%)
    pallas_call x1, Pallas kernels, exchange(): pl.pallas_call(exchange_kernel, out_shape=(pltpu.VMEM((2, 512, 512), F32)...  53 us
    pallas_call x1, Pallas kernels, halo(): pl.pallas_call(halo_kernel, out_shape=tuple(outs) + (jax.ShapeDtypeStruct...  27.7 us
    pallas_call x1, Pallas kernels, compute(): pl.pallas_call(compute_kernel, out_shape=(pltpu.VMEM((2, 776, 896), jnp.f...  12.3 us
    pallas_call x1, Pallas kernels, finish(): pl.pallas_call(finish_kernel, out_shape=(pltpu.HBM(new_obj.shape, F32), p...  3.14 us

profile of v5, /device:TPU:1, one launch (start us, length us, event | category | flops | bytes accessed | tf_op | source)
XLA Modules:
  0.0 96.9 jit_solution(8320499800787449162)
XLA Ops:
  0.6 0.0 copy-start
  0.6 0.0 copy-start.1
  0.7 27.7 %halo.1 = (f32[2,776,896]{2,1,0:T(8,128)S(1)}, f32[2,4,256,256]{3,2,1,0:T(8,128)S(1)}, f32[4,2,256,128]{3,2,1,0:T(8,128)S(1)}, bf16[2,256,768]{2,1,0:T(8,128)(2,...) custom-call(f32[2,512,512]{2,1,0:T(8,128)} %obj.1, ...), custom_call_target="tpu_custom_call" | custom-call | tf_op jit(solution)/shard_map/halo/pallas_call | solution.py:426
  28.4 0.0 copy-done
  28.4 0.0 copy-done.1
  28.4 12.3 %compute.1 = (f32[2,776,896]{2,1,0:T(8,128)S(1)}, f32[2,4,256,256]{3,2,1,0:T(8,128)S(1)}, f32[8,128]{1,0:T(8,128)S(1)}) custom-call(s32[128]{0:T(128)S(1)} %copy-done.1, s32[1,2,4]{2,1,0:T(2,128)S(1)} %bitcast.7, f32[2,776,896]{2,1,0:T(8,128)S(1)} %get-tuple-element.22.ext.obj, ...), custom_call_target="tpu_custom_call", output_to_operand_aliasing={{0}: (9, {}), {1}: (10, {})} | custom-call | tf_op jit(solution)/shard_map/compute/pallas_call | solution.py:230
  40.7 53.0 %exchange.1 = (f32[2,512,512]{2,1,0:T(8,128)S(1)}, f32[2048,256]{1,0:T(8,128)S(1)}, f32[1,1]{1,0:T(1,128)}) custom-call(f32[2,776,896]{2,1,0:T(8,128)S(1)} %get-tuple-element.31.gext, f32[2048,256]{1,0:T(8,128)S(1)} %bitcast.6, f32[2,776,896]{2,1,0:T(8,128)S(1)} %get-tuple-element.22.ext.obj, f32[2048,256]{1,0:T(8,128)S(1)} %bitcast.5, ...), custom_call_target="tpu_custom_call" | custom-call | tf_op jit(solution)/shard_map/exchange/pallas_call | solution.py:635
  93.8 3.1 %finish.1 = (f32[2,512,512]{2,1,0:T(8,128)}, f32[2048,256]{1,0:T(8,128)}, f32[1,1]{1,0:T(1,128)}) custom-call(f32[2,512,512]{2,1,0:T(8,128)S(1)} %get-tuple-element.35.new_obj, f32[2048,256]{1,0:T(8,128)S(1)} %get-tuple-element.36.new_probe, f32[1,1]{1,0:T(1,128)} %get-tuple-element.37.loss_mean), custom_call_target="tpu_custom_call" | custom-call | tf_op jit(solution)/shard_map/finish/pallas_call | solution.py:683
Async XLA Ops:
  0.6 27.7 %copy-start = (s32[1,4,2]{1,2,0:T(2,128)S(1)}, s32[1,4,2]{1,2,0:T(2,128)}, u32[]{:S(2)}) copy-start(s32[1,4,2]{1,2,0:T(2,128)} %param.13) | copy-start | bytes 100
  0.6 27.7 %copy-start.1 = (s32[128]{0:T(128)S(1)}, s32[128]{0:T(128)}, u32[]{:S(2)}) copy-start(s32[128]{0:T(128)} %counts.1) | copy-start | bytes 1540

commit v6 on v5

--- a/solution.py
+++ b/solution.py
@@ -445,8 +445,8 @@
 PARTS = ((0, 128, "xyz"), (128, 128, "yzx"), (256, 128, "zxy"), (384, 256, "xyz"), (640, 128, "yzx"), (768, 256, "zxy"))
 
 
-def exchange_kernel(gext, pg, obj, probe, peak, loss, new_obj, new_probe, loss_mean,
-                    strip, corner, over, side, relay, r0, r1, r2, rz, value, slots, send, recv):
+def exchange_kernel(gext, pg, probe, peak, loss, over, side, inverse, new_probe, loss_mean,
+                    strip, corner, relay, r0, r1, r2, rz, value, slots, send, recv):
     n = 256
     left, right, above, below = neighbours()
     group = groups()
@@ -601,8 +601,7 @@
     push_over(3)
     push_side(5)
     probe_peak = jnp.max(sum(probe[m * n : (m + 1) * n] * probe[m * n : (m + 1) * n] for m in range(8)))
-    inverse = 1.0 / probe_peak
-    new_obj[:, n : 2 * n, n : 2 * n] = obj[:, n : 2 * n, n : 2 * n] - gext[:, n : 2 * n, n : 2 * n] * inverse
+    inverse[...] = jnp.full((8, 128), 1.0 / probe_peak, F32)
     final = []
     for p, (first, size, axes) in enumerate(PARTS):
         q = size // 4
@@ -617,35 +616,32 @@
             sent += copies
     for copy in over_sent:
         copy.wait_recv()
-    new_obj[:, 0:n, n : 2 * n] = obj[:, 0:n, n : 2 * n] - (gext[:, 0:n, n : 2 * n] + over[:, :, n : 2 * n]) * inverse
     for copy in side_sent + rounds[2]:
         copy.wait_recv()
     sent += over_sent + side_sent + rounds[0] + rounds[1] + rounds[2] + corner_sent + swap + final + small.done
-    new_obj[:, 0:n, 0:n] = obj[:, 0:n, 0:n] - (gext[:, 0:n, 0:n] + over[:, :, 0:n] + side[:, 0:n]) * inverse
-    new_obj[:, n : 2 * n, 0:n] = obj[:, n : 2 * n, 0:n] - (gext[:, n : 2 * n, 0:n] + side[:, n : 2 * n]) * inverse
     for copy in final:
         copy.wait_recv()
     for copy in sent:
         copy.wait_send()
 
 
-def exchange(gext, pg, obj, probe, peak, loss):
+def exchange(gext, pg, probe, peak, loss):
     V = pl.BlockSpec(memory_space=pltpu.VMEM)
     S = pl.BlockSpec(memory_space=pltpu.SMEM)
-    new_obj, new_probe, loss_mean = pl.pallas_call(
+    return pl.pallas_call(
         exchange_kernel,
         out_shape=(
-            pltpu.VMEM((2, 512, 512), F32),
+            pltpu.VMEM((2, 256, 512), F32),
+            pltpu.VMEM((2, 512, 256), F32),
+            pltpu.VMEM((8, 128), F32),
             pltpu.VMEM((2048, 256), F32),
             jax.ShapeDtypeStruct((1, 1), F32),
         ),
-        in_specs=[V] * 6,
-        out_specs=(V, V, S),
+        in_specs=[V] * 5,
+        out_specs=(V, V, V, V, S),
         scratch_shapes=[
             pltpu.VMEM((2, 256, 256), F32),
             pltpu.VMEM((2, 256, 256), F32),
-            pltpu.VMEM((2, 256, 512), F32),
-            pltpu.VMEM((2, 512, 256), F32),
             pltpu.VMEM((2, 2, 2, 64, 256), F32),
             pltpu.VMEM((1024, 256), F32),
             pltpu.VMEM((3, 256, 256), F32),
@@ -658,41 +654,50 @@
         ],
         compiler_params=pltpu.CompilerParams(collective_id=1, has_side_effects=True, vmem_limit_bytes=30 << 20),
         name="exchange",
-    )(gext, pg.reshape(2048, 256), obj, probe.reshape(2048, 256), peak, loss)
-    return new_obj, new_probe, loss_mean
-
-
-def finish_kernel(new_obj, new_probe, loss_mean, obj_out, probe_out, loss_out, sems):
+    )(gext, pg.reshape(2048, 256), probe.reshape(2048, 256), peak, loss)
+
+
+def finish_kernel(gext, obj, over, side, inverse, new_probe, loss_mean, obj_out, probe_out, loss_out, new_obj, sems):
+    n = 256
     copies = []
     for i in range(4):
-        m = pl.ds(128 * i, 128)
-        copies.append(pltpu.make_async_copy(new_obj.at[:, m], obj_out.at[:, m], sems.at[i]))
         m = pl.ds(512 * i, 512)
         copies.append(pltpu.make_async_copy(new_probe.at[m], probe_out.at[m], sems.at[4 + i]))
-    for copy in copies:
-        copy.start()
+        copies[-1].start()
     loss_out[0, 0] = loss_mean[0, 0]
+    scale = inverse[0:1, 0:1]
+    for i in range(4):
+        m = pl.ds(128 * i, 128)
+        left = gext[:, m, 0:n] + side[:, m]
+        right = gext[:, m, n : 2 * n]
+        if i < 2:
+            left += over[:, m, 0:n]
+            right += over[:, m, n : 2 * n]
+        new_obj[:, m, 0:n] = obj[:, m, 0:n] - left * scale
+        new_obj[:, m, n : 2 * n] = obj[:, m, n : 2 * n] - right * scale
+        copies.append(pltpu.make_async_copy(new_obj.at[:, m], obj_out.at[:, m], sems.at[i]))
+        copies[-1].start()
     for copy in copies:
         copy.wait()
 
 
-def finish(new_obj, new_probe, loss_mean):
+def finish(gext, obj, over, side, inverse, new_probe, loss_mean):
     V = pl.BlockSpec(memory_space=pltpu.VMEM)
     A = pl.BlockSpec(memory_space=pltpu.HBM)
     S = pl.BlockSpec(memory_space=pltpu.SMEM)
     return pl.pallas_call(
         finish_kernel,
         out_shape=(
-            pltpu.HBM(new_obj.shape, F32),
+            pltpu.HBM((2, 512, 512), F32),
             pltpu.HBM(new_probe.shape, F32),
             jax.ShapeDtypeStruct((1, 1), F32),
         ),
-        in_specs=[V, V, S],
+        in_specs=[V] * 6 + [S],
         out_specs=(A, A, S),
-        scratch_shapes=[pltpu.SemaphoreType.DMA((8,))],
-        compiler_params=pltpu.CompilerParams(vmem_limit_bytes=6 << 20),
+        scratch_shapes=[pltpu.VMEM((2, 512, 512), F32), pltpu.SemaphoreType.DMA((8,))],
+        compiler_params=pltpu.CompilerParams(vmem_limit_bytes=8 << 20),
         name="finish",
-    )(new_obj, new_probe, loss_mean)
+    )(gext, obj, over, side, inverse, new_probe, loss_mean)
 
 
 def body(object_slab, probe_field, patterns, offsets, counts):
@@ -700,7 +705,7 @@
     gext, pg, loss = compute(
         counts, jnp.swapaxes(offsets, 1, 2), ext, probe, pats, left, left_t, right, right_t, gext, pg
     )
-    new_obj, new_probe, loss_mean = finish(*exchange(gext, pg, ext, probe, peak, loss))
+    new_obj, new_probe, loss_mean = finish(gext, ext, *exchange(gext, pg, probe, peak, loss))
     return new_obj, new_probe.reshape(probe_field.shape), loss_mean.reshape(())
 
 

time: 96.3 us -> 97.1 us (level); the launches traced: 96.9 us -> 96.6 us
    pallas_call x1, Pallas kernels: 12.3 us -> 7.09 us  [compute(): pl.pallas_call(compute_kernel, out_shape=(pltpu.VMEM((2, 776, 896), jnp.f...]
    pallas_call x2, Pallas kernels: 56.2 us -> 61.1 us  [the longest x1 58 us: exchange(): pl.pallas_call(exchange_kernel, out_shape=(pltpu.VMEM((2, 256, 512), F32)...]
where the time goes in v6:
time: 97.1 us; the launch traced here: 96.6 us
  Pallas kernels  95.9 us (99%)
    pallas_call x1, Pallas kernels, exchange(): pl.pallas_call(exchange_kernel, out_shape=(pltpu.VMEM((2, 256, 512), F32)...  58 us
    pallas_call x1, Pallas kernels, halo(): pl.pallas_call(halo_kernel, out_shape=tuple(outs) + (jax.ShapeDtypeStruct...  27.7 us
    pallas_call x1, Pallas kernels, compute(): pl.pallas_call(compute_kernel, out_shape=(pltpu.VMEM((2, 776, 896), jnp.f...  7.09 us
    pallas_call x1, Pallas kernels, finish(): pl.pallas_call(finish_kernel, out_shape=(pltpu.HBM((2, 512, 512), F32), p...  3.14 us

profile of v6, /device:TPU:1, one launch (start us, length us, event | category | flops | bytes accessed | tf_op | source)
XLA Modules:
  0.0 96.6 jit_solution(7954260171598505658)
XLA Ops:
  0.6 0.0 copy-start
  0.6 0.0 copy-start.1
  0.7 27.7 %halo.1 = (f32[2,776,896]{2,1,0:T(8,128)S(1)}, f32[2,4,256,256]{3,2,1,0:T(8,128)S(1)}, f32[4,2,256,128]{3,2,1,0:T(8,128)S(1)}, bf16[2,256,768]{2,1,0:T(8,128)(2,...) custom-call(f32[2,512,512]{2,1,0:T(8,128)} %obj.1, ...), custom_call_target="tpu_custom_call" | custom-call | tf_op jit(solution)/shard_map/halo/pallas_call | solution.py:426
  28.4 0.0 copy-done
  28.4 0.0 copy-done.1
  28.4 7.1 %compute.1 = (f32[2,776,896]{2,1,0:T(8,128)S(1)}, f32[2,4,256,256]{3,2,1,0:T(8,128)S(1)}, f32[8,128]{1,0:T(8,128)S(1)}) custom-call(s32[128]{0:T(128)S(1)} %copy-done.1, s32[1,2,4]{2,1,0:T(2,128)S(1)} %bitcast.7, f32[2,776,896]{2,1,0:T(8,128)S(1)} %get-tuple-element.24.ext.obj, ...), custom_call_target="tpu_custom_call", output_to_operand_aliasing={{0}: (9, {}), {1}: (10, {})} | custom-call | tf_op jit(solution)/shard_map/compute/pallas_call | solution.py:230
  35.5 58.0 %exchange.1 = (f32[2,256,512]{2,1,0:T(8,128)S(1)}, f32[2,512,256]{2,1,0:T(8,128)S(1)}, f32[8,128]{1,0:T(8,128)S(1)}, f32[2048,256]{1,0:T(8,128)S(1)}, f32[1,1]{1,0:T(1,128)}) custom-call(f32[2,776,896]{2,1,0:T(8,128)S(1)} %get-tuple-element.33.gext, f32[2048,256]{1,0:T(8,128)S(1)} %bitcast.6, f32[2048,256]{1,0:T(8,128)S(1)} %bitcast.5, ...), custom_call_target="tpu_custom_call" | custom-call | tf_op jit(solution)/shard_map/exchange/pallas_call | solution.py:631
  93.5 3.1 %finish.1 = (f32[2,512,512]{2,1,0:T(8,128)}, f32[2048,256]{1,0:T(8,128)}, f32[1,1]{1,0:T(1,128)}) custom-call(f32[2,776,896]{2,1,0:T(8,128)S(1)} %get-tuple-element.33.gext, f32[2,776,896]{2,1,0:T(8,128)S(1)} %get-tuple-element.24.ext.obj, f32[2,256,512]{2,1,0:T(8,128)S(1)} %get-tuple-element.37.over, f32[2,512,256]{2,1,0:T(8,128)S(1)} %get-tuple-element.38.side, ...), custom_call_target="tpu_custom_call" | custom-call | tf_op jit(solution)/shard_map/finish/pallas_call | solution.py:688
Async XLA Ops:
  0.6 27.7 %copy-start = (s32[1,4,2]{1,2,0:T(2,128)S(1)}, s32[1,4,2]{1,2,0:T(2,128)}, u32[]{:S(2)}) copy-start(s32[1,4,2]{1,2,0:T(2,128)} %param.13) | copy-start | bytes 100
  0.6 27.7 %copy-start.1 = (s32[128]{0:T(128)S(1)}, s32[128]{0:T(128)}, u32[]{:S(2)}) copy-start(s32[128]{0:T(128)} %counts.1) | copy-start | bytes 1540
